TPU v7x, 256 devices: a whole 4x4x8 slice. The times are simulated.
256 devices in a mesh: dp: 4 (over y), row: 4 (over z_hi, core), col: 16 (over x, z_lo).
Axes of the slice: x: 4, y: 4, z: 8 (z_hi: 2, z_lo: 4; z = z_hi * 4 + z_lo), core: 2. Of those that a mesh axis runs over, the one named last changes fastest.
Arguments:
- features: bfloat16 [8, 256, 6144], P('dp', 'row', 'col'), may hold values from -6 to 6
- ln_gain: float32 [6144], P('col'), may hold values from 0.5 to 10, as said below
- w_qkv: bfloat16 [6144, 3, 3072], P('col', None, 'row'), may hold values from -0.078125 to 0.078125
- qk_gain: float32 [2, 128], replicated, may hold values from 0.25 to 1.75
- w_up: bfloat16 [6144, 12288], P('col', 'row'), may hold values from -1 to 1
- w_out: bfloat16 [3072, 6144], P('row', 'col'), may hold values from -0.109375 to 0.109375
- w_down: bfloat16 [12288, 6144], P('row', 'col'), may hold values from -0.0546875 to 0.0546875
- cotangent: bfloat16 [8, 256, 6144], P('dp', 'row', 'col'), may hold values from -6 to 6
Outputs:
- output: bfloat16 [8, 256, 6144], P('dp', 'row', 'col')
- input_grad: bfloat16 [8, 256, 6144], P('dp', 'row', 'col')
- ln_grad: float32 [6144], P('col')
- gain_grads: float32 [2, 128], replicated
- qkv_grad: float32 [6144, 3, 3072], P('col', None, ('row', 'dp'))
- up_grad: float32 [6144, 12288], P('col', ('row', 'dp'))
- out_grad: float32 [3072, 6144], P(('row', 'dp'), 'col')
- down_grad: float32 [12288, 6144], P(('row', 'dp'), 'col')
Inputs may be any that keep to these rules, and one draw needn't show every extreme that they name: `ln_gain`: positive gains.
All inputs are finite; a program needn't handle non-finite values.
Results may differ from a plain program's by a relative error of at most 0.034.
Values may be sent and summed in bfloat16 or wider, within the bound.
A program may use at most 128 MiB of HBM per device.

v0:
```python
import jax
import jax.numpy as jnp
from jax import lax
from jax.sharding import PartitionSpec as P

EPS = 1e-06
SQRT_HALF = 0.7071067811865476
INV_ROOT = 0.3989422804014327


def gelu_value(values):
    return 0.5 * values * (1.0 + jax.scipy.special.erf(values * SQRT_HALF))


def gelu_slope(values):
    return (
        0.5 * (1.0 + jax.scipy.special.erf(values * SQRT_HALF))
        + values * jnp.exp(-0.5 * values * values) * INV_ROOT
    )


def normalize(values):
    average = jnp.mean(values, -1, keepdims=True)
    spread = jnp.mean(values * values, -1, keepdims=True) - average * average
    factor = lax.rsqrt(spread + EPS)
    return ((values - average) * factor, factor)


def norm_back(grad_normed, normed, factor, gain):
    scaled = grad_normed * gain
    centre = jnp.mean(scaled, -1, keepdims=True)
    along = jnp.mean(scaled * normed, -1, keepdims=True)
    return factor * (scaled - centre - normed * along)


def on_device(features, ln_gain, w_qkv, qk_gain, w_up, w_out, w_down, cotangent):
    images_here, row_patches, col_width = features.shape
    patch_total = row_patches * lax.axis_size("row")
    col_patches = patch_total // lax.axis_size("col")
    head_cols = w_qkv.shape[2]
    head_size = qk_gain.shape[1]
    heads_here = head_cols // head_size
    width = col_width * lax.axis_size("col")
    qkv_flat = w_qkv.reshape(col_width, 3 * head_cols)
    inputs_wide = features.astype(jnp.float32)
    first_sums, square_sums = lax.psum(
        (jnp.sum(inputs_wide, -1), jnp.sum(inputs_wide * inputs_wide, -1)), "col"
    )
    average = (first_sums / width)[..., None]
    spread = (square_sums / width)[..., None] - average * average
    factor = lax.rsqrt(spread + EPS)
    normed = (inputs_wide - average) * factor
    scaled_in = (normed * ln_gain).astype(jnp.bfloat16)
    gathered_in = lax.all_gather(scaled_in, "row", axis=1, tiled=True)
    piece = gathered_in
    first = jnp.einsum("bpd,dx->pbx", piece, qkv_flat, preferred_element_type=jnp.float32)
    second = jnp.einsum("bpd,df->pbf", piece, w_up, preferred_element_type=jnp.float32)
    inner = lax.psum_scatter(
        jnp.concatenate([first, second], -1), "col", scatter_dimension=0, tiled=True
    )
    projected = inner[..., : 3 * head_cols].reshape(
        col_patches, images_here, 3, heads_here, head_size
    )
    hidden_pre = inner[..., 3 * head_cols :]
    query_hat, query_factor = normalize(projected[:, :, 0])
    key_hat, key_factor = normalize(projected[:, :, 1])
    query_half = (query_hat * qk_gain[0]).astype(jnp.bfloat16)
    key_half = (key_hat * qk_gain[1]).astype(jnp.bfloat16)
    value_half = projected[:, :, 2].astype(jnp.bfloat16)
    key_all, value_all = (
        lax.all_gather(key_half, "col", axis=0, tiled=True),
        lax.all_gather(value_half, "col", axis=0, tiled=True),
    )
    scale = head_size ** (-0.5)
    scores = (
        jnp.einsum("qbhd,kbhd->bhqk", query_half, key_all, preferred_element_type=jnp.float32)
        * scale
    )
    expo = jnp.exp(scores)
    weights = expo / jnp.sum(expo, -1, keepdims=True)
    weights_half = weights.astype(jnp.bfloat16)
    attended = jnp.einsum(
        "bhqk,kbhd->qbhd", weights_half, value_all, preferred_element_type=jnp.float32
    )
    attended = attended.astype(jnp.bfloat16).reshape(col_patches, images_here, head_cols)
    hidden = gelu_value(hidden_pre).astype(jnp.bfloat16)
    attended_all = lax.all_gather(attended, "col", axis=0, tiled=True)
    hidden_all = lax.all_gather(hidden, "col", axis=0, tiled=True)
    first = jnp.einsum("pbx,xd->bpd", attended_all, w_out, preferred_element_type=jnp.float32)
    second = jnp.einsum("pbf,fd->bpd", hidden_all, w_down, preferred_element_type=jnp.float32)
    mixed = lax.psum_scatter(
        jnp.transpose(first + second, (1, 0, 2)).astype(jnp.bfloat16),
        "row",
        scatter_dimension=0,
        tiled=True,
    ).astype(jnp.float32)
    output = (inputs_wide + jnp.transpose(mixed, (1, 0, 2))).astype(jnp.bfloat16)
    grad_all = lax.all_gather(cotangent, "row", axis=1, tiled=True)
    piece = grad_all
    first = jnp.einsum("bpd,xd->pbx", piece, w_out, preferred_element_type=jnp.float32)
    second = jnp.einsum("bpd,fd->pbf", piece, w_down, preferred_element_type=jnp.float32)
    backward = lax.psum_scatter(
        jnp.concatenate([first, second], -1).astype(jnp.bfloat16),
        "col",
        scatter_dimension=0,
        tiled=True,
    ).astype(jnp.float32)
    attn_grad = (
        backward[..., :head_cols]
        .astype(jnp.bfloat16)
        .reshape(col_patches, images_here, heads_here, head_size)
    )
    pre_grad = (backward[..., head_cols:] * gelu_slope(hidden_pre)).astype(jnp.bfloat16)
    weight_grad = jnp.einsum(
        "qbhd,kbhd->bhqk", attn_grad, value_all, preferred_element_type=jnp.float32
    )
    score_grad = (
        weights * (weight_grad - jnp.sum(weights * weight_grad, -1, keepdims=True))
    ).astype(jnp.bfloat16)
    query_grad = (
        jnp.einsum("bhqk,kbhd->qbhd", score_grad, key_all, preferred_element_type=jnp.float32)
        * scale
    )
    key_part = (
        jnp.einsum("bhqk,qbhd->kbhd", score_grad, query_half, preferred_element_type=jnp.float32)
        * scale
    )
    value_part = jnp.einsum(
        "bhqk,qbhd->kbhd", weights_half, attn_grad, preferred_element_type=jnp.float32
    )
    key_grad, value_grad = (
        lax.psum_scatter(
            key_part.astype(jnp.bfloat16), "col", scatter_dimension=0, tiled=True
        ).astype(jnp.float32),
        lax.psum_scatter(
            value_part.astype(jnp.bfloat16), "col", scatter_dimension=0, tiled=True
        ).astype(jnp.float32),
    )
    gain_terms = jnp.stack(
        [jnp.sum(query_grad * query_hat, (0, 1, 2)), jnp.sum(key_grad * key_hat, (0, 1, 2))]
    )
    query_back = norm_back(query_grad, query_hat, query_factor, qk_gain[0])
    key_back = norm_back(key_grad, key_hat, key_factor, qk_gain[1])
    proj_grad = jnp.stack([query_back, key_back, value_grad], 2).astype(jnp.bfloat16)
    proj_grad = proj_grad.reshape(col_patches, images_here, 3, head_cols)
    proj_all, pre_all = (
        lax.all_gather(proj_grad, "col", axis=0, tiled=True),
        lax.all_gather(pre_grad, "col", axis=0, tiled=True),
    )
    first = jnp.einsum("pbtx,dtx->bpd", proj_all, w_qkv, preferred_element_type=jnp.float32)
    second = jnp.einsum("pbf,df->bpd", pre_all, w_up, preferred_element_type=jnp.float32)
    norm_grad = jnp.transpose(
        lax.psum_scatter(
            jnp.transpose(first + second, (1, 0, 2)).astype(jnp.bfloat16),
            "row",
            scatter_dimension=0,
            tiled=True,
        ).astype(jnp.float32),
        (1, 0, 2),
    )
    scaled_grad = norm_grad * ln_gain
    centre_sum, along_sum = lax.psum(
        (jnp.sum(scaled_grad, -1), jnp.sum(scaled_grad * normed, -1)), "col"
    )
    centre = (centre_sum / width)[..., None]
    along = (along_sum / width)[..., None]
    input_grad = (
        cotangent.astype(jnp.float32) + factor * (scaled_grad - centre - normed * along)
    ).astype(jnp.bfloat16)
    ln_grad = lax.psum(jnp.sum(norm_grad * normed, (0, 1)), ("dp", "row"))
    gain_grads = lax.psum(gain_terms, ("dp", "row", "col"))
    qkv_local = jnp.einsum(
        "bpd,pbtx->dtx", gathered_in, proj_all, preferred_element_type=jnp.float32
    )
    up_local = jnp.einsum("bpd,pbf->df", gathered_in, pre_all, preferred_element_type=jnp.float32)
    out_local = jnp.einsum(
        "pbx,bpd->xd", attended_all, grad_all, preferred_element_type=jnp.float32
    )
    down_local = jnp.einsum("pbf,bpd->fd", hidden_all, grad_all, preferred_element_type=jnp.float32)
    qkv_grad, up_grad, out_grad, down_grad = (
        lax.psum_scatter(
            qkv_local.astype(jnp.bfloat16), "dp", scatter_dimension=2, tiled=True
        ).astype(jnp.float32),
        lax.psum_scatter(
            up_local.astype(jnp.bfloat16), "dp", scatter_dimension=1, tiled=True
        ).astype(jnp.float32),
        lax.psum_scatter(
            out_local.astype(jnp.bfloat16), "dp", scatter_dimension=0, tiled=True
        ).astype(jnp.float32),
        lax.psum_scatter(
            down_local.astype(jnp.bfloat16), "dp", scatter_dimension=0, tiled=True
        ).astype(jnp.float32),
    )
    return (output, input_grad, ln_grad, gain_grads, qkv_grad, up_grad, out_grad, down_grad)


def solution(mesh):
    in_specs = (
        P("dp", "row", "col"),
        P("col"),
        P("col", None, "row"),
        P(),
        P("col", "row"),
        P("row", "col"),
        P("row", "col"),
        P("dp", "row", "col"),
    )
    out_specs = (
        P("dp", "row", "col"),
        P("dp", "row", "col"),
        P("col"),
        P(),
        P("col", None, ("row", "dp")),
        P("col", ("row", "dp")),
        P(("row", "dp"), "col"),
        P(("row", "dp"), "col"),
    )
    return jax.shard_map(
        on_device, mesh=mesh, in_specs=in_specs, out_specs=out_specs, check_vma=False
    )
```

profile of v0, /device:TPU:1, one launch (start us, length us, event | category | flops | bytes accessed | tf_op | source)
XLA Modules:
  0.0 1205.7 jit_solution(13517612641614124918)
XLA Ops:
  8.4 38.4 %all-reduce.2 = (f32[2,64]{1,0:T(2,128)S(1)}, f32[2,64]{1,0:T(2,128)S(1)}) all-reduce(f32[2,64]{1,0:T(2,128)S(1)} %get-tuple-element.17, f32[2,64]{1,0:T(2,128)S(1)} %get-tuple-element.16), channel_id=1, replica_groups=mesh['dp'=4,'row'=4,'col'=16] {'col'}, use_global_device_ids=true, to_apply=%region_3.0 | all-reduce | flops 256 | bytes 2048 | tf_op jit(solution)/shard_map/psum | solution.py:46
  48.4 18.6 %all_gather.24 = bf16[2,256,384]{2,1,0:T(8,128)(2,1)S(1)} all-gather(bf16[2,64,384]{2,1,0:T(8,128)(2,1)S(1)} %fusion.42), channel_id=1, replica_groups=mesh['dp'=4,'row'=4,'col'=16] {'row'}, dimensions={1}, use_global_device_ids=true | all-gather | bytes 491520 | tf_op jit(solution)/shard_map/all_gather | solution.py:54
  70.9 5.0 convolution_bitcast_fusion.1
  80.4 9.0 pad_maximum_fusion
  90.3 11.6 all_gather.29
  110.6 216.2 %reduce-scatter.10.cloned.1.call-done = f32[16,2,5376]{2,0,1:T(8,128)} async-done(((f32[256,2,5376]{2,0,1:T(8,128)}), f32[16,2,5376]{2,0,1:T(8,128)}) %reduce-scatter.10.cloned.1.call-update) | async-done | bytes 688144 | tf_op jit(solution)/shard_map/reduce_scatter | solution.py:58
  330.7 55.3 %all_gather.26 = bf16[256,2,6,128]{3,0,2,1:T(8,128)(2,1)} all-gather(bf16[16,2,6,128]{3,0,2,1:T(8,128)(2,1)S(1)} %multiply_convert_fusion.3), channel_id=1, replica_groups=mesh['dp'=4,'row'=4,'col'=16] {'col'}, dimensions={0}, use_global_device_ids=true | all-gather | bytes 835584 | tf_op jit(solution)/shard_map/all_gather | solution.py:71
  386.0 56.1 %all-gather = bf16[256,2,1,6,128]{4,0,3,1,2:T(8,128)(2,1)S(1)} all-gather(bf16[16,2,1,6,128]{4,0,3,1,2:T(8,128)(2,1)S(1)} %copy.121), channel_id=2, replica_groups=mesh['dp'=4,'row'=4,'col'=16] {'col'}, dimensions={0}, use_global_device_ids=true | all-gather | bytes 835584 | tf_op jit(solution)/shard_map/all_gather | solution.py:72
  442.1 9.4 reduce-scatter.14.cloned.1.call-done
  473.6 139.7 %all-reduce.5.cloned.1.call-done = bf16[256,2,6,128]{3,1,2,0:T(2,128)(2,1)} async-done(((bf16[256,2,6,128]{3,1,2,0:T(2,128)(2,1)}), bf16[256,2,6,128]{3,1,2,0:T(2,128)(2,1)}) %all-reduce.5.cloned.1.call-update) | async-done | bytes 786448
  616.3 83.7 %reduce-scatter.16.cloned.1.call-done = bf16[16,2,6,128]{3,0,2,1:T(8,128)(2,1)} async-done(((bf16[256,2,6,128]{3,0,2,1:T(8,128)(2,1)}), bf16[16,2,6,128]{3,0,2,1:T(8,128)(2,1)}) %reduce-scatter.16.cloned.1.call-update) | async-done | bytes 49168 | tf_op jit(solution)/shard_map/reduce_scatter | solution.py:132
  710.1 42.3 %all_gather.27 = bf16[256,2,768]{2,0,1:T(8,128)(2,1)S(1)} all-gather(bf16[16,2,768]{2,0,1:T(8,128)(2,1)S(1)} %bitcast.189), channel_id=1, replica_groups=mesh['dp'=4,'row'=4,'col'=16] {'col'}, dimensions={0}, use_global_device_ids=true | all-gather | bytes 835584 | tf_op jit(solution)/shard_map/all_gather | solution.py:87
  755.0 41.1 %all-gather.7.cloned.1.call-done = bf16[256,2,3,768]{3,0,2,1:T(8,128)(2,1)} async-done(((bf16[16,2,3,768]{3,0,2,1:T(8,128)(2,1)}), bf16[256,2,3,768]{3,0,2,1:T(8,128)(2,1)}) %all-gather.7.cloned.1.call-update) | async-done | bytes 2359312 | tf_op jit(solution)/shard_map/all_gather | solution.py:147
  796.2 4.5 fusion.11
  800.6 89.9 %all-gather.9.cloned.1.call-done = bf16[256,2,3072]{2,0,1:T(8,128)(2,1)} async-done(((bf16[16,2,3072]{2,0,1:T(8,128)(2,1)}), bf16[256,2,3072]{2,0,1:T(8,128)(2,1)}) %all-gather.9.cloned.1.call-update) | async-done | bytes 3145744 | tf_op jit(solution)/shard_map/all_gather | solution.py:148
  890.5 4.7 fusion.19
  895.3 87.2 %all-gather.5.cloned.1.call-done = bf16[256,2,3072]{2,0,1:T(8,128)(2,1)} async-done(((bf16[16,2,3072]{2,0,1:T(8,128)(2,1)}), bf16[256,2,3072]{2,0,1:T(8,128)(2,1)}) %all-gather.5.cloned.1.call-update) | async-done | bytes 3145744 | tf_op jit(solution)/shard_map/all_gather | solution.py:88
  992.8 4.7 bitcast_convert_fusion.1
  998.5 5.2 bitcast_convert_fusion
  1003.7 10.5 reduce-scatter.24.cloned.1.call-done
  1015.8 79.6 %psum.47 = f32[2,128]{1,0:T(2,128)} all-reduce(f32[2,128]{1,0:T(2,128)S(1)} %pad_maximum_fusion.3), channel_id=1, replica_groups=mesh['dp'=4,'row'=4,'col'=16] {'dp','row','col'}, use_global_device_ids=true, to_apply=%region_28.0 | all-reduce | flops 256 | bytes 2048 | tf_op jit(solution)/shard_map/psum | solution.py:171
  1096.6 32.6 %all-reduce.1 = (f32[2,64]{1,0:T(2,128)S(1)}, f32[2,64]{1,0:T(2,128)S(1)}) all-reduce(f32[2,64]{1,0:T(2,128)S(1)} %get-tuple-element.11, f32[2,64]{1,0:T(2,128)S(1)} %get-tuple-element.14), channel_id=1, replica_groups=mesh['dp'=4,'row'=4,'col'=16] {'col'}, use_global_device_ids=true, to_apply=%region_23.0 | all-reduce | flops 256 | bytes 2048 | tf_op jit(solution)/shard_map/psum | solution.py:162
  1129.2 51.0 %psum.46 = f32[384]{0:T(512)} all-reduce(f32[384]{0:T(512)S(1)} %get-tuple-element.10), channel_id=1, replica_groups=mesh['dp'=4,'row'=4,'col'=16] {'dp','row'}, use_global_device_ids=true, to_apply=%region_25.0 | all-reduce | flops 384 | bytes 3072 | tf_op jit(solution)/shard_map/psum | solution.py:170
  1186.1 11.0 reduce-scatter.26.cloned.1.call-done
  (129 shorter events, 83.6 us)
Async XLA Ops:
  7.2 68.8 %copy-start = (bf16[384,3072]{1,0:T(8,128)(2,1)S(1)}, bf16[384,3072]{1,0:T(8,128)(2,1)}, u32[]{:S(2)}) copy-start(bf16[384,3072]{1,0:T(8,128)(2,1)} %param.12) | copy-start | bytes 7077892
  7.2 319.7 %reduce-scatter.10.cloned.1.call-start = ((), (), s32[]{:S(2)}) async-start(), calls=%async_computation.9 | async-start | bytes 11698176 | tf_op jit(solution)/shard_map/reduce_scatter | solution.py:58
  89.4 362.0 %reduce-scatter.14.cloned.1.call-start = ((), (), s32[]{:S(2)}) async-start(), calls=%async_computation.12 | async-start | bytes 4177920 | tf_op jit(solution)/shard_map/reduce_scatter | solution.py:102
  101.9 1.8 copy-start.4
  109.5 503.8 %all-reduce.5.cloned.1.call-start = ((), (), s32[]{:S(2)}) async-start(), calls=%async_computation.21 | async-start | bytes 1572864
  110.6 219.6 %copy-start.17 = (f32[128]{0:T(128)}, f32[128]{0:T(128)S(1)}, u32[]{:S(2)}) copy-start(f32[128]{0:T(128)S(1)} %get-tuple-element.34) | copy-start | bytes 1540
  461.5 238.5 %reduce-scatter.16.cloned.1.call-start = ((), (), s32[]{:S(2)}) async-start(), calls=%async_computation.13 | async-start | bytes 835584 | tf_op jit(solution)/shard_map/reduce_scatter | solution.py:132
  465.7 330.5 %all-gather.7.cloned.1.call-start = ((), (), s32[]{:S(2)}) async-start(), calls=%async_computation.14 | async-start | bytes 2506752 | tf_op jit(solution)/shard_map/all_gather | solution.py:147
  706.1 184.5 %all-gather.9.cloned.1.call-start = ((), (), s32[]{:S(2)}) async-start(), calls=%async_computation.15 | async-start | bytes 3342336 | tf_op jit(solution)/shard_map/all_gather | solution.py:148
  708.1 274.3 %all-gather.5.cloned.1.call-start = ((), (), s32[]{:S(2)}) async-start(), calls=%async_computation.10 | async-start | bytes 3342336 | tf_op jit(solution)/shard_map/all_gather | solution.py:88
  708.9 305.3 %reduce-scatter.24.cloned.1.call-start = ((), (), s32[]{:S(2)}) async-start(), calls=%async_computation.19 | async-start | bytes 737280 | tf_op jit(solution)/shard_map/reduce_scatter | solution.py:187
  754.8 340.6 %reduce-scatter.18.cloned.1.call-start = ((), (), s32[]{:S(2)}) async-start(), calls=%async_computation.16 | async-start | bytes 491520 | tf_op jit(solution)/shard_map/reduce_scatter | solution.py:153
  895.2 284.9 %reduce-scatter.12.cloned.1.call-start = ((), (), s32[]{:S(2)}) async-start(), calls=%async_computation.11 | async-start | bytes 491520 | tf_op jit(solution)/shard_map/reduce_scatter | solution.py:91
  982.5 4.5 copy-start.3
  988.3 193.6 %reduce-scatter.20.cloned.1.call-start = ((), (), s32[]{:S(2)}) async-start(), calls=%async_computation.17 | async-start | bytes 2211840 | tf_op jit(solution)/shard_map/reduce_scatter | solution.py:181
  992.7 191.2 %reduce-scatter.22.cloned.1.call-start = ((), (), s32[]{:S(2)}) async-start(), calls=%async_computation.18 | async-start | bytes 2949120 | tf_op jit(solution)/shard_map/reduce_scatter | solution.py:184
  997.5 1.0 copy-start.5
  997.5 199.5 %reduce-scatter.26.cloned.1.call-start = ((), (), s32[]{:S(2)}) async-start(), calls=%async_computation.20 | async-start | bytes 2949120 | tf_op jit(solution)/shard_map/reduce_scatter | solution.py:190
  1003.7 12.2 %copy-start.18 = (f32[128]{0:T(128)S(1)}, f32[128]{0:T(128)}, u32[]{:S(2)}) copy-start(f32[128]{0:T(128)} %get-tuple-element.8) | copy-start | bytes 1540
  1003.7 91.8 %copy-start.6 = (bf16[2,64,384]{2,1,0:T(8,128)(2,1)S(1)}, bf16[2,64,384]{2,1,0:T(8,128)(2,1)}, u32[]{:S(2)}) copy-start(bf16[2,64,384]{2,1,0:T(8,128)(2,1)} %param.8) | copy-start | bytes 294916
  1003.7 91.8 %copy-start.12 = (f32[384]{0:T(512)S(1)}, f32[384]{0:T(512)}, u32[]{:S(2)}) copy-start(f32[384]{0:T(512)} %param.9) | copy-start | bytes 4612
  1003.7 91.8 %copy-start.14 = (f32[2,64]{1,0:T(2,128)S(1)}, f32[2,64]{1,0:T(2,128)}, u32[]{:S(2)}) copy-start(f32[2,64]{1,0:T(2,128)} %copy-done.13) | copy-start | bytes 1540
  1003.7 91.8 %copy-start.16 = (f32[2,64]{1,0:T(2,128)S(1)}, f32[2,64]{1,0:T(2,128)}, u32[]{:S(2)}) copy-start(f32[2,64]{1,0:T(2,128)} %copy-done.15) | copy-start | bytes 1540
  1003.7 176.5 %copy-start.9 = (bf16[2,64,384]{2,1,0:T(8,128)(2,1)S(1)}, bf16[2,64,384]{2,1,0:T(8,128)(2,1)}, u32[]{:S(2)}) copy-start(bf16[2,64,384]{2,1,0:T(8,128)(2,1)} %param.15) | copy-start | bytes 294916
  (9 other events, 5.9 us)
Sparse Core Ops, SparseCore 0:
  89.5 237.2 reduce-scatter.9
  329.4 121.9 reduce-scatter.13
  461.6 151.5 all-reduce.4
  616.2 83.7 reduce-scatter.15
  706.2 89.9 all-gather.6
  798.5 91.9 all-gather.8
  892.5 89.9 all-gather.4
  985.7 28.4 reduce-scatter.23
  1017.7 39.2 reduce-scatter.17
  1060.4 34.2 reduce-scatter.11
  1097.5 25.9 reduce-scatter.19
  1125.9 34.2 reduce-scatter.21
  1162.8 34.2 reduce-scatter.25
where the time goes:
time: 1210 us
  waiting for transfers between devices  690 us (57%)
  blocking collectives  385 us (32%)
  matrix products  58.8 us (5%)
  other arithmetic  33.4 us (3%)
  local copies, waits for them, and re-layouts  22.9 us (2%)
  between operations  14.9 us (1%)
    reduce_scatter x1, waiting for transfers between devices, on_device(): lax.psum_scatter(jnp.concatenate([first, second], -1), 'col', scatter_dim...  216 us
    unnamed x14, waiting for transfers between devices  141 us
    all_gather x1, waiting for transfers between devices, on_device(): lax.all_gather(pre_grad, 'col', axis=0, tiled=True)  89.9 us
    all_gather x1, waiting for transfers between devices, on_device(): hidden_all = lax.all_gather(hidden, 'col', axis=0, tiled=True)  87.2 us
    reduce_scatter x1, waiting for transfers between devices, on_device(): lax.psum_scatter(key_part.astype(jnp.bfloat16), 'col', scatter_dimension=...  83.7 us
    psum x1, blocking collectives, on_device(): gain_grads = lax.psum(gain_terms, ('dp', 'row', 'col'))  79.6 us
    all_gather x1, blocking collectives, on_device(): lax.all_gather(value_half, 'col', axis=0, tiled=True)  56.1 us
    all_gather x1, blocking collectives, on_device(): lax.all_gather(key_half, 'col', axis=0, tiled=True)  55.3 us
  transfers between devices with their start and end apart: 13, of which 9 were waited for; matrix products, arithmetic and copies ran while one was open for 6% of the time, Pallas kernels for 0%

commit v1 on v0

v1 whole, which is shorter than its diff:
```python
import functools

import jax
import jax.numpy as jnp
from jax import lax
from jax.experimental import pallas as pl
from jax.experimental.pallas import tpu as pltpu
from jax.sharding import PartitionSpec as P

EPS = 1e-06
SQRT_HALF = 0.7071067811865476
INV_ROOT = 0.3989422804014327
HEAD = 128
SIDE = 4
PIECES = 9
MESH = pl.DeviceIdType.MESH
F32 = jnp.float32
BF16 = jnp.bfloat16


def gelu_both(values):
    cdf = 0.5 * (1.0 + lax.erf(values * SQRT_HALF))
    slope = cdf + values * jnp.exp(-0.5 * values * values) * INV_ROOT
    return values * cdf, slope


def normalize(values):
    average = jnp.mean(values, -1, keepdims=True)
    spread = jnp.mean(values * values, -1, keepdims=True) - average * average
    factor = lax.rsqrt(spread + EPS)
    return ((values - average) * factor, factor)


def norm_back(grad_normed, normed, factor, gain):
    scaled = grad_normed * gain
    centre = jnp.mean(scaled, -1, keepdims=True)
    along = jnp.mean(scaled * normed, -1, keepdims=True)
    return factor * (scaled - centre - normed * along)


def dot(a, b):
    return lax.dot_general(a, b, (((1,), (0,)), ((), ())), preferred_element_type=F32)


def dot_nt(a, b):
    return lax.dot_general(a, b, (((1,), (1,)), ((), ())), preferred_element_type=F32)


def exact_nt(a, b):
    return lax.dot_general(
        a,
        b,
        (((1,), (1,)), ((), ())),
        precision=lax.Precision.HIGHEST,
        preferred_element_type=F32,
    )


def greet(peers):
    barrier = pltpu.get_barrier_semaphore()
    for peer in peers:
        pl.semaphore_signal(barrier, inc=1, device_id=peer, device_id_type=MESH)
    pl.semaphore_wait(barrier, len(peers))


def remote(src, dst, send, recv, peer):
    return pltpu.make_async_remote_copy(
        src_ref=src,
        dst_ref=dst,
        send_sem=send,
        recv_sem=recv,
        device_id=peer,
        device_id_type=MESH,
    )


def pre_kernel(
    rows, cols, x_ref, gain_ref, cot_ref,
    xin_ref, call_ref, avg_ref, factor_ref,
    mine, stats, stat_send, stat_recv, row_send, row_recv,
):
    dp, row, col = lax.axis_index("dp"), lax.axis_index("row"), lax.axis_index("col")
    images, patches, width = x_ref.shape
    tokens = images * patches

    def col_peer(k):
        return (dp, row, lax.rem(col + k, cols))

    def row_peer(k):
        return (dp, lax.rem(row + k, rows), col)

    greet([col_peer(k) for k in range(1, cols)] + [row_peer(k) for k in range(1, rows)])
    here = pl.ds(pl.multiple_of(row * patches, patches), patches)
    sends = []
    for k in range(1, rows):
        copy = remote(
            cot_ref, call_ref.at[:, here, :], row_send.at[0, k - 1], row_recv.at[0, k - 1], row_peer(k)
        )
        copy.start()
        sends.append(copy)
    x = x_ref[...].astype(F32).reshape(tokens, width)
    ones = jnp.ones((8, width), F32)
    first = exact_nt(ones, x)
    second = exact_nt(ones, x * x)
    which = lax.broadcasted_iota(jnp.int32, (8, tokens), 0)
    local = jnp.where(which == 0, first, second)
    mine[...] = local
    stat_copies = []
    for k in range(1, cols):
        copy = remote(mine, stats.at[k - 1], stat_send.at[k - 1], stat_recv.at[k - 1], col_peer(k))
        copy.start()
        stat_copies.append(copy)
    call_ref[:, here, :] = cot_ref[...]
    total = local
    for k in range(1, cols):
        stat_copies[k - 1].wait_recv()
        total = total + stats[k - 1]
    total = total * (1.0 / (width * cols))
    average = total[0:1]
    factor = lax.rsqrt(total[1:2] - average * average + EPS)
    both = jnp.where(which == 0, average, factor)
    eye = (
        lax.broadcasted_iota(jnp.int32, (tokens, tokens), 0)
        == lax.broadcasted_iota(jnp.int32, (tokens, tokens), 1)
    ).astype(F32)
    turned = exact_nt(eye, both)
    avg_col, factor_col = turned[:, 0:1], turned[:, 1:2]
    normed = (x - avg_col) * factor_col
    xin_ref[:, here, :] = (normed * gain_ref[...]).astype(BF16).reshape(images, patches, width)
    for k in range(1, rows):
        copy = remote(
            xin_ref.at[:, here, :],
            xin_ref.at[:, here, :],
            row_send.at[1, k - 1],
            row_recv.at[1, k - 1],
            row_peer(k),
        )
        copy.start()
        sends.append(copy)
    avg_ref[...] = jnp.broadcast_to(avg_col, avg_ref.shape)
    factor_ref[...] = jnp.broadcast_to(factor_col, factor_ref.shape)
    for copy in sends:
        copy.wait_recv()
    for copy in sends + stat_copies:
        copy.wait_send()


def vmem(count):
    return [pl.BlockSpec(memory_space=pltpu.VMEM)] * count


def gather_inputs(features, ln_gain, cotangent):
    rows, cols = lax.axis_size("row"), lax.axis_size("col")
    images, patches, width = features.shape
    tokens = images * patches
    whole = jax.ShapeDtypeStruct((images, patches * rows, width), BF16)
    column = jax.ShapeDtypeStruct((tokens, HEAD), F32)
    return pl.pallas_call(
        functools.partial(pre_kernel, rows, cols),
        out_shape=(whole, whole, column, column),
        in_specs=vmem(3),
        out_specs=tuple(vmem(4)),
        scratch_shapes=[
            pltpu.VMEM((8, tokens), F32),
            pltpu.VMEM((cols - 1, 8, tokens), F32),
            pltpu.SemaphoreType.DMA((cols - 1,)),
            pltpu.SemaphoreType.DMA((cols - 1,)),
            pltpu.SemaphoreType.DMA((2, max(rows - 1, 1))),
            pltpu.SemaphoreType.DMA((2, max(rows - 1, 1))),
        ],
        compiler_params=pltpu.CompilerParams(collective_id=0, has_side_effects=True),
        name="gather_inputs",
    )(features, ln_gain.reshape(1, width), cotangent)


def owner_z(piece):
    return piece if piece < 3 else piece - 3 if piece < 6 else 3


def owner_slot(piece):
    return 0 if piece < 3 else 1 if piece < 6 else piece - 6


def core_kernel(
    x_ref, c_ref, wq_ref, wup_ref, wout_ref, wdown_ref, gain_ref,
    g_ref, gains_ref,
    opp, right_send, left_send, right_acc, left_acc, own,
    half_left, half_right, full_left, full_right, z_send, z_recv,
    s_opp, r_half, s_side, r_full, s_z, r_z, s_own, r_own, s_fwd, r_fwd, s_zag, r_zag,
):
    dp, row, col = lax.axis_index("dp"), lax.axis_index("row"), lax.axis_index("col")
    xi, zi = col // SIDE, lax.rem(col, SIDE)
    xr, xl, xo = lax.rem(xi + 1, SIDE), lax.rem(xi + 3, SIDE), lax.rem(xi + 2, SIDE)
    right, left = (dp, row, xr * SIDE + zi), (dp, row, xl * SIDE + zi)

    def z_peer(k):
        return (dp, row, xi * SIDE + lax.rem(zi + k, SIDE))

    greet([right, left] + [z_peer(k) for k in range(1, SIDE)])

    def partial_block(block, emit):
        image, run = block // 2, lax.rem(block, 2)
        triple = pl.ds(pl.multiple_of(run * 3 * HEAD, 3 * HEAD), 3 * HEAD)
        for part in range(3):
            start = part * 6 * HEAD + run * 3 * HEAD
            values = dot(x_ref[image], wq_ref[:, pl.ds(pl.multiple_of(start, HEAD), 3 * HEAD)])
            for z in range(3):
                emit(z, part, values[:, z * HEAD : (z + 1) * HEAD])
        values = dot_nt(c_ref[image], wout_ref[triple, :])
        for z in range(3):
            emit(z, 3, values[:, z * HEAD : (z + 1) * HEAD])
        hidden = pl.ds(pl.multiple_of(block * 6 * HEAD, 6 * HEAD), 6 * HEAD)
        for im in range(2):
            values = dot(x_ref[im], wup_ref[:, hidden])
            for j in range(6):
                emit(3 + j, im, values[:, j * HEAD : (j + 1) * HEAD])
            values = dot_nt(c_ref[im], wdown_ref[hidden, :])
            for j in range(6):
                emit(3 + j, 2 + im, values[:, j * HEAD : (j + 1) * HEAD])

    low, high = pl.ds(0, 2), pl.ds(2, 2)

    def opp_right(p):
        return remote(opp.at[p, low], half_left.at[p], s_opp.at[0, p], r_half.at[0, p], right)

    def opp_left(p):
        return remote(opp.at[p, high], half_right.at[p], s_opp.at[1, p], r_half.at[1, p], left)

    def side_right(p, half):
        part = pl.ds(2 * half, 2)
        return remote(
            right_send.at[p, part],
            full_left.at[p, part],
            s_side.at[0, half, p],
            r_full.at[0, half, p],
            right,
        )

    def side_left(p, half):
        part = pl.ds(2 * half, 2)
        return remote(
            left_send.at[p, part],
            full_right.at[p, part],
            s_side.at[1, half, p],
            r_full.at[1, half, p],
            left,
        )

    def emit_opp(p, part, values):
        opp[p, part] = values.astype(BF16)

    partial_block(xo, emit_opp)
    for p in range(PIECES):
        opp_right(p).start()
        opp_left(p).start()

    def emit_right(p, part, values):
        if part >= 2:
            right_send[p, part] = values.astype(BF16)
        else:
            right_acc[p, part] = values

    partial_block(xr, emit_right)
    for p in range(PIECES):
        side_right(p, 1).start()

    def emit_left(p, part, values):
        if part < 2:
            left_send[p, part] = values.astype(BF16)
        else:
            left_acc[p, part - 2] = values

    partial_block(xl, emit_left)
    for p in range(PIECES):
        side_left(p, 0).start()

    def emit_own(p, part, values):
        own[p, part] = values

    partial_block(xi, emit_own)

    def pass_on(p, carry):
        opp_right(p).wait_recv()
        right_send[p, low] = (right_acc[p] + half_left[p].astype(F32)).astype(BF16)
        side_right(p, 0).start()
        opp_left(p).wait_recv()
        left_send[p, high] = (left_acc[p] + half_right[p].astype(F32)).astype(BF16)
        side_left(p, 1).start()
        return carry

    lax.fori_loop(0, PIECES, pass_on, 0)

    def z_copy(p, k):
        return remote(
            z_send.at[p],
            z_recv.at[k - 1, owner_slot(p)],
            s_z.at[p],
            r_z.at[k - 1, owner_slot(p)],
            z_peer(k),
        )

    for p in range(PIECES):
        for half in range(2):
            side_right(p, half).wait_recv()
            side_left(p, half).wait_recv()
        own[p] = own[p] + full_left[p].astype(F32) + full_right[p].astype(F32)
        for k in range(1, SIDE):

            @pl.when(lax.rem(zi + k, SIDE) == owner_z(p))
            def _():
                z_send[p] = own[p].astype(BF16)
                z_copy(p, k).start()

    def arrived(p, slot):
        total = own[p]
        for k in range(1, SIDE):
            remote(
                z_send.at[0], z_recv.at[k - 1, slot], s_z.at[0], r_z.at[k - 1, slot], z_peer(k)
            ).wait_recv()
            total = total + z_recv[k - 1, slot].astype(F32)
        return total

    def own_ag(p, way):
        peer = right if way == 0 else left
        return remote(g_ref.at[xi, p], g_ref.at[xi, p], s_own.at[way, p], r_own.at[way, p], peer)

    def z_ag(p, k):
        return remote(g_ref.at[xi, p], g_ref.at[xi, p], s_zag.at[k - 1, p], r_zag.at[p], z_peer(k))

    def launch(p):
        for way in range(2):
            own_ag(p, way).start()
        for k in range(1, SIDE):
            z_ag(p, k).start()

    def hidden_units(p, slot):
        total = arrived(p, slot)
        for im in range(2):
            value, slope = gelu_both(total[im])
            g_ref[xi, p, im] = value.astype(BF16)
            g_ref[xi, p, 2 + im] = (total[2 + im] * slope).astype(BF16)
        launch(p)

    scale = HEAD ** (-0.5)

    def attention(p):
        total = arrived(p, 0)
        query_hat, query_factor = normalize(total[0])
        key_hat, key_factor = normalize(total[1])
        query_gain, key_gain = gain_ref[0:1, :], gain_ref[1:2, :]
        query = (query_hat * query_gain).astype(BF16)
        key = (key_hat * key_gain).astype(BF16)
        value = total[2].astype(BF16)
        grad = total[3].astype(BF16)
        expo = jnp.exp(dot_nt(query, key) * scale)
        weights = expo / jnp.sum(expo, -1, keepdims=True)
        weights_half = weights.astype(BF16)
        g_ref[xi, p, 0] = dot(weights_half, value).astype(BF16)
        weight_grad = dot_nt(grad, value)
        score_grad = weights * (weight_grad - jnp.sum(weights * weight_grad, -1, keepdims=True))
        score_grad = score_grad.astype(BF16)
        query_grad = dot(score_grad, key) * scale
        key_grad = dot(score_grad.T, query) * scale
        value_grad = dot(weights_half.T, grad)
        gains_ref[0:1, :] = jnp.sum(query_grad * query_hat, 0, keepdims=True)
        gains_ref[1:2, :] = jnp.sum(key_grad * key_hat, 0, keepdims=True)
        g_ref[xi, p, 1] = norm_back(query_grad, query_hat, query_factor, query_gain).astype(BF16)
        g_ref[xi, p, 2] = norm_back(key_grad, key_hat, key_factor, key_gain).astype(BF16)
        g_ref[xi, p, 3] = value_grad.astype(BF16)
        launch(p)

    gains_ref[...] = jnp.zeros_like(gains_ref)

    @pl.when(zi < 3)
    def _():
        hidden_units(zi + 3, 1)
        attention(zi)

    @pl.when(zi == 3)
    def _():
        for j in range(3):
            hidden_units(6 + j, j)

    def fwd_copy(p, way):
        block = xl if way == 0 else xr
        part = low if way == 0 else high
        there = right if way == 0 else left
        return remote(
            g_ref.at[block, p, part],
            g_ref.at[block, p, part],
            s_fwd.at[way, p],
            r_fwd.at[way, p],
            there,
        )

    def each_piece(step, body):
        z = lax.rem(zi + step, SIDE)

        @pl.when(z < 3)
        def _():
            body(z + 3)
            body(z)

        @pl.when(z == 3)
        def _():
            for j in range(3):
                body(6 + j)

    def spread(p):
        z_ag(p, 1).wait_recv()
        for way in range(2):
            own_ag(p, way).start()

    def relay(p):
        for way in range(2):
            own_ag(p, way).wait_recv()
            fwd_copy(p, way).start()

    each_piece(1, spread)
    each_piece(0, relay)
    each_piece(2, spread)
    each_piece(1, relay)
    each_piece(3, spread)
    each_piece(2, relay)
    each_piece(3, relay)

    def finish(p, carry):
        opp_right(p).wait_send()
        opp_left(p).wait_send()
        for half in range(2):
            side_right(p, half).wait_send()
            side_left(p, half).wait_send()
        for way in range(2):
            own_ag(p, way).wait_send()
            fwd_copy(p, way).wait()
        return carry

    lax.fori_loop(0, PIECES, finish, 0)
    for p in range(PIECES):

        @pl.when(zi != owner_z(p))
        def _():
            z_copy(p, 1).wait_send()

        @pl.when(zi == owner_z(p))
        def _():
            for k in range(1, SIDE):
                z_ag(p, k).wait_send()


def exchange(x_all, c_all, w_qkv, w_up, w_out, w_down, qk_gain):
    images, patches, width = x_all.shape
    piece = (4, patches, HEAD)
    half = (2, patches, HEAD)
    dma = pltpu.SemaphoreType.DMA
    return pl.pallas_call(
        core_kernel,
        out_shape=(
            jax.ShapeDtypeStruct((SIDE, PIECES) + piece, BF16),
            jax.ShapeDtypeStruct((8, HEAD), F32),
        ),
        in_specs=vmem(7),
        out_specs=tuple(vmem(2)),
        scratch_shapes=[
            pltpu.VMEM((PIECES,) + piece, BF16),
            pltpu.VMEM((PIECES,) + piece, BF16),
            pltpu.VMEM((PIECES,) + piece, BF16),
            pltpu.VMEM((PIECES,) + half, F32),
            pltpu.VMEM((PIECES,) + half, F32),
            pltpu.VMEM((PIECES,) + piece, F32),
            pltpu.VMEM((PIECES,) + half, BF16),
            pltpu.VMEM((PIECES,) + half, BF16),
            pltpu.VMEM((PIECES,) + piece, BF16),
            pltpu.VMEM((PIECES,) + piece, BF16),
            pltpu.VMEM((PIECES,) + piece, BF16),
            pltpu.VMEM((SIDE - 1, 3) + piece, BF16),
            dma((2, PIECES)),
            dma((2, PIECES)),
            dma((2, 2, PIECES)),
            dma((2, 2, PIECES)),
            dma((PIECES,)),
            dma((SIDE - 1, 3)),
            dma((2, PIECES)),
            dma((2, PIECES)),
            dma((2, PIECES)),
            dma((2, PIECES)),
            dma((SIDE - 1, PIECES)),
            dma((PIECES,)),
        ],
        compiler_params=pltpu.CompilerParams(
            collective_id=1, has_side_effects=True, vmem_limit_bytes=60 * 1024 * 1024
        ),
        name="exchange",
    )(x_all, c_all, w_qkv, w_up, w_out, w_down, qk_gain)


def on_device(features, ln_gain, w_qkv, qk_gain, w_up, w_out, w_down, cotangent):
    images, patches, width = features.shape
    head_cols = w_qkv.shape[2]
    total_width = width * lax.axis_size("col")
    x_all, c_all, average, factor = gather_inputs(features, ln_gain, cotangent)
    qkv_flat = w_qkv.reshape(width, 3 * head_cols)
    pieces, gains = exchange(x_all, c_all, qkv_flat, w_up, w_out, w_down, qk_gain)
    every = pieces.shape[3]
    inputs_wide = features.astype(F32)
    average = average[:, :1].reshape(images, patches, 1)
    factor = factor[:, :1].reshape(images, patches, 1)
    normed = (inputs_wide - average) * factor

    def heads_of(part):
        values = pieces[:, 0:3, part].reshape(2, 2, 3, every, HEAD)
        return jnp.transpose(values, (0, 3, 1, 2, 4)).reshape(images, every, head_cols)

    def units_of(first):
        values = pieces[:, 3:9, first : first + 2]
        return jnp.transpose(values, (2, 3, 0, 1, 4)).reshape(images, every, 6 * SIDE * HEAD)

    attended_all = heads_of(0)
    proj_all = jnp.concatenate([heads_of(1), heads_of(2), heads_of(3)], -1)
    hidden_all, pre_all = units_of(0), units_of(2)

    def row_sum(first, second):
        return lax.psum_scatter(
            (first + second).astype(BF16), "row", scatter_dimension=1, tiled=True
        ).astype(F32)

    def ein(spec, a, b):
        return jnp.einsum(spec, a, b, preferred_element_type=F32)

    mixed = row_sum(
        ein("bpx,xd->bpd", attended_all, w_out), ein("bpf,fd->bpd", hidden_all, w_down)
    )
    output = (inputs_wide + mixed).astype(BF16)
    norm_grad = row_sum(
        ein("bpx,dx->bpd", proj_all, qkv_flat), ein("bpf,df->bpd", pre_all, w_up)
    )
    scaled_grad = norm_grad * ln_gain
    centre_sum, along_sum = lax.psum(
        (jnp.sum(scaled_grad, -1), jnp.sum(scaled_grad * normed, -1)), "col"
    )
    centre = (centre_sum / total_width)[..., None]
    along = (along_sum / total_width)[..., None]
    input_grad = (
        cotangent.astype(F32) + factor * (scaled_grad - centre - normed * along)
    ).astype(BF16)
    ln_grad = lax.psum(jnp.sum(norm_grad * normed, (0, 1)), ("dp", "row"))
    gain_grads = lax.psum(gains[:2], ("dp", "row", "col"))

    def dp_sum(values, dim):
        return lax.psum_scatter(
            values.astype(BF16), "dp", scatter_dimension=dim, tiled=True
        ).astype(F32)

    qkv_grad = dp_sum(ein("bpd,bpx->dx", x_all, proj_all).reshape(width, 3, head_cols), 2)
    up_grad = dp_sum(ein("bpd,bpf->df", x_all, pre_all), 1)
    out_grad = dp_sum(ein("bpx,bpd->xd", attended_all, c_all), 0)
    down_grad = dp_sum(ein("bpf,bpd->fd", hidden_all, c_all), 0)
    return (output, input_grad, ln_grad, gain_grads, qkv_grad, up_grad, out_grad, down_grad)


def solution(mesh):
    in_specs = (
        P("dp", "row", "col"),
        P("col"),
        P("col", None, "row"),
        P(),
        P("col", "row"),
        P("row", "col"),
        P("row", "col"),
        P("dp", "row", "col"),
    )
    out_specs = (
        P("dp", "row", "col"),
        P("dp", "row", "col"),
        P("col"),
        P(),
        P("col", None, ("row", "dp")),
        P("col", ("row", "dp")),
        P(("row", "dp"), "col"),
        P(("row", "dp"), "col"),
    )
    return jax.shard_map(
        on_device, mesh=mesh, in_specs=in_specs, out_specs=out_specs, check_vma=False
    )
```

time: 1210 us -> 533 us (0.44)
  waiting for transfers between devices: 690 us -> 1.37 us
  Pallas kernels: 0 us -> 238 us
  blocking collectives: 385 us -> 199 us
  matrix products: 58.8 us -> 26 us
  other arithmetic: 33.4 us -> 10.9 us
  local copies, waits for them, and re-layouts: 22.9 us -> 41.9 us
    reduce_scatter x9 -> x6, waiting for transfers between devices: 331 us -> 1.27 us  [the longest x4 1.27 us: dp_sum(): lax.psum_scatter(values.astype(BF16), 'dp', scatter_dimension=dim, tiled=...]
    pallas_call x0 -> x2, Pallas kernels: none -> 238 us  [the longest x1 208 us: exchange(): pl.pallas_call(core_kernel, out_shape=(jax.ShapeDtypeStruct((SIDE, PIECES...]
    all_gather x3 -> x0, waiting for transfers between devices: 218 us -> none  [the longest x1 89.9 us: on_device(): lax.all_gather(pre_grad, 'col', axis=0, tiled=True)]
    all_gather x5 -> x0, blocking collectives: 184 us -> none  [the longest x1 56.1 us: on_device(): lax.all_gather(value_half, 'col', axis=0, tiled=True)]
    unnamed x14 -> x6, waiting for transfers between devices: 141 us -> 0.1 us
    dot_general x17 -> x8, matrix products: 55.8 us -> 26 us  [ein(): return jnp.einsum(spec, a, b, preferred_element_type=F32)]
    psum x2 -> x1, blocking collectives: 118 us -> 114 us  [on_device(): gain_grads = lax.psum(gains[:2], ('dp', 'row', 'col'))]
  transfers between devices with their start and end apart: 13 -> 6, of which waited for: 9 -> 1; matrix products, arithmetic and copies ran while one was open for 6% -> 7% of each run, Pallas kernels for 0% -> 0%
where the time goes in v1:
time: 533 us; the launch traced here: 532 us
  Pallas kernels  238 us (45%)
  blocking collectives  199 us (37%)
  local copies, waits for them, and re-layouts  41.9 us (8%)
  matrix products  26 us (5%)
  between operations  14.3 us (3%)
  other arithmetic  10.9 us (2%)
    pallas_call x1, Pallas kernels, exchange(): pl.pallas_call(core_kernel, out_shape=(jax.ShapeDtypeStruct((SIDE, PIECES...  208 us
    psum x1, blocking collectives, on_device(): gain_grads = lax.psum(gains[:2], ('dp', 'row', 'col'))  114 us
    psum x1, blocking collectives, on_device(): ln_grad = lax.psum(jnp.sum(norm_grad * normed, (0, 1)), ('dp', 'row'))  51 us
    psum x1, blocking collectives, on_device(): lax.psum((jnp.sum(scaled_grad, -1), jnp.sum(scaled_grad * normed, -1)), '...  34.4 us
    pallas_call x1, Pallas kernels, gather_inputs(): pl.pallas_call(functools.partial(pre_kernel, rows, cols), out_shape=(whol...  30.2 us
    dot_general x8, matrix products, ein(): return jnp.einsum(spec, a, b, preferred_element_type=F32)  26 us
    transpose x3, local copies, waits for them, and re-layouts, units_of(): jnp.transpose(values, (2, 3, 0, 1, 4))  11.1 us
  transfers between devices with their start and end apart: 6, of which 1 were waited for; matrix products, arithmetic and copies ran while one was open for 7% of the time, Pallas kernels for 0%

profile of v1, /device:TPU:1, one launch (start us, length us, event | category | flops | bytes accessed | tf_op | source)
XLA Modules:
  0.0 532.3 jit_solution(16121922087624026537)
XLA Ops:
  8.5 2.8 copy.26
  11.2 2.4 copy.27.wq_ref
  13.7 30.2 %gather_inputs.1 = (bf16[2,256,384]{2,1,0:T(8,128)(2,1)}, bf16[2,256,384]{2,1,0:T(8,128)(2,1)}, f32[128,128]{1,0:T(8,128)}, f32[128,128]{1,0:T(8,128)}) custom-call(bf16[2,64,384]{2,1,0:T(8,128)(2,1)} %x_ref.1, f32[1,384]{1,0:T(1,128)} %reshape.49.gain_ref, bf16[2,64,384]{2,1,0:T(8,128)(2,1)} %cot_ref.1), custom_call_target="tpu_custom_call" | custom-call | tf_op jit(solution)/shard_map/gather_inputs/pallas_call | solution.py:158
  43.9 207.8 %exchange.1 = (bf16[4,9,4,256,128]{4,3,2,1,0:T(8,128)(2,1)}, f32[8,128]{1,0:T(8,128)}) custom-call(bf16[2,256,384]{2,1,0:T(8,128)(2,1)} %get-tuple-element.14.x_ref, bf16[2,256,384]{2,1,0:T(8,128)(2,1)} %get-tuple-element.15.c_ref, bf16[384,2304]{1,0:T(8,128)(2,1)} %copy.27.wq_ref, bf16[384,3072]{1,0:T(8,128)(2,1)} %wup_ref.1, bf16[768,384]{1,0:T(8,128)(2,1)} %wout_ref.1, ...), custom_call_target="tpu_custom_call" | custom-call | tf_op jit(solution)/shard_map/exchange/pallas_call | solution.py:456
  251.7 3.6 fusion.29
  255.3 5.1 slice_bitcast_fusion
  260.4 2.3 copy.32
  262.7 2.3 copy.35
  265.0 2.3 copy.33
  267.3 2.3 copy.36
  271.8 2.3 copy.37
  274.1 2.8 copy.38
  276.9 3.7 fusion.13
  280.8 2.7 fusion.9
  284.7 3.2 copy.30
  287.9 3.6 fusion.3
  293.0 2.5 fusion.5
  295.6 4.1 fusion
  299.7 3.9 copy.41
  303.6 4.9 bitcast_convert_fusion.1
  308.8 3.2 bitcast_convert_fusion
  313.9 114.0 %psum.31 = f32[2,128]{1,0:T(2,128)} all-reduce(f32[2,128]{1,0:T(2,128)S(1)} %slice.35), channel_id=1, replica_groups=mesh['dp'=4,'row'=4,'col'=16] {'dp','row','col'}, use_global_device_ids=true, to_apply=%region_8.0 | all-reduce | flops 256 | bytes 2048 | tf_op jit(solution)/shard_map/psum | solution.py:547
  429.0 34.4 %all-reduce = (f32[2,64]{1,0:T(2,128)S(1)}, f32[2,64]{1,0:T(2,128)S(1)}) all-reduce(f32[2,64]{1,0:T(2,128)S(1)} %get-tuple-element.21, f32[2,64]{1,0:T(2,128)S(1)} %get-tuple-element.22), channel_id=1, replica_groups=mesh['dp'=4,'row'=4,'col'=16] {'col'}, use_global_device_ids=true, to_apply=%region_5.0 | all-reduce | flops 256 | bytes 2048 | tf_op jit(solution)/shard_map/psum | solution.py:538
  463.4 51.0 %psum.30 = f32[384]{0:T(512)} all-reduce(f32[384]{0:T(512)S(1)} %get-tuple-element.20), channel_id=1, replica_groups=mesh['dp'=4,'row'=4,'col'=16] {'dp','row'}, use_global_device_ids=true, to_apply=%region_7.0 | all-reduce | flops 384 | bytes 3072 | tf_op jit(solution)/shard_map/psum | solution.py:546
  (50 shorter events, 20.8 us)
Async XLA Ops:
  7.2 420.7 %reduce-scatter.9.cloned.1.call-start = ((), (), s32[]{:S(2)}) async-start(), calls=%async_computation.7 | async-start | bytes 491520 | tf_op jit(solution)/shard_map/reduce_scatter | solution.py:523
  11.2 240.5 %copy-start = (bf16[384,3,768]{0,2,1:T(8,128)(2,1)}, bf16[384,3,768]{0,2,1:T(8,128)(2,1)S(1)}, u32[]{:S(2)}) copy-start(bf16[384,3,768]{0,2,1:T(8,128)(2,1)S(1)} %copy.26) | copy-start | bytes 5308420
  276.9 3.7 copy-start.3
  276.9 3.9 copy-start.5
  280.8 2.7 copy-start.2
  283.5 230.9 %reduce-scatter.7.cloned.1.call-start = ((), (), s32[]{:S(2)}) async-start(), calls=%async_computation.6 | async-start | bytes 491520 | tf_op jit(solution)/shard_map/reduce_scatter | solution.py:523
  287.9 3.6 copy-start.1
  287.9 3.6 copy-start.4
  287.9 5.1 copy-start.6
  293.0 223.2 %reduce-scatter.15.cloned.1.call-start = ((), (), s32[]{:S(2)}) async-start(), calls=%async_computation.10 | async-start | bytes 737280 | tf_op jit(solution)/shard_map/reduce_scatter | solution.py:550
  295.6 222.3 %reduce-scatter.11.cloned.1.call-start = ((), (), s32[]{:S(2)}) async-start(), calls=%async_computation.8 | async-start | bytes 2211840 | tf_op jit(solution)/shard_map/reduce_scatter | solution.py:550
  303.6 216.3 %reduce-scatter.13.cloned.1.call-start = ((), (), s32[]{:S(2)}) async-start(), calls=%async_computation.9 | async-start | bytes 2949120 | tf_op jit(solution)/shard_map/reduce_scatter | solution.py:550
  308.5 119.3 %copy-start.7 = (f32[384]{0:T(512)S(1)}, f32[384]{0:T(512)}, u32[]{:S(2)}) copy-start(f32[384]{0:T(512)} %param.9) | copy-start | bytes 4612
  308.6 214.7 %reduce-scatter.17.cloned.1.call-start = ((), (), s32[]{:S(2)}) async-start(), calls=%async_computation.11 | async-start | bytes 2949120 | tf_op jit(solution)/shard_map/reduce_scatter | solution.py:550
Sparse Core Ops, SparseCore 0:
  283.6 73.8 reduce-scatter.8
  360.2 34.2 reduce-scatter.6
  397.1 18.5 reduce-scatter.14
  418.1 31.2 reduce-scatter.10
  452.0 34.2 reduce-scatter.12
  488.8 34.3 reduce-scatter.16

commit v2 on v1

v2 whole, which is shorter than its diff:
```python
import functools

import jax
import jax.numpy as jnp
from jax import lax
from jax.experimental import pallas as pl
from jax.experimental.pallas import tpu as pltpu
from jax.sharding import PartitionSpec as P

EPS = 1e-06
SQRT_HALF = 0.7071067811865476
INV_ROOT = 0.3989422804014327
HEAD = 128
SIDE = 4
PIECES = 9
MESH = pl.DeviceIdType.MESH
VMEM_BYTES = 62 * 1024 * 1024
F32 = jnp.float32
BF16 = jnp.bfloat16


def gelu_both(values):
    cdf = 0.5 * (1.0 + lax.erf(values * SQRT_HALF))
    slope = cdf + values * jnp.exp(-0.5 * values * values) * INV_ROOT
    return values * cdf, slope


def normalize(values):
    average = jnp.mean(values, -1, keepdims=True)
    spread = jnp.mean(values * values, -1, keepdims=True) - average * average
    factor = lax.rsqrt(spread + EPS)
    return ((values - average) * factor, factor)


def norm_back(grad_normed, normed, factor, gain):
    scaled = grad_normed * gain
    centre = jnp.mean(scaled, -1, keepdims=True)
    along = jnp.mean(scaled * normed, -1, keepdims=True)
    return factor * (scaled - centre - normed * along)


def dot(a, b):
    return lax.dot_general(a, b, (((1,), (0,)), ((), ())), preferred_element_type=F32)


def dot_nt(a, b):
    return lax.dot_general(a, b, (((1,), (1,)), ((), ())), preferred_element_type=F32)


def exact_nt(a, b):
    return lax.dot_general(
        a,
        b,
        (((1,), (1,)), ((), ())),
        precision=lax.Precision.HIGHEST,
        preferred_element_type=F32,
    )


def greet(peers):
    barrier = pltpu.get_barrier_semaphore()
    for peer in peers:
        pl.semaphore_signal(barrier, inc=1, device_id=peer, device_id_type=MESH)
    pl.semaphore_wait(barrier, len(peers))


def remote(src, dst, send, recv, peer):
    return pltpu.make_async_remote_copy(
        src_ref=src,
        dst_ref=dst,
        send_sem=send,
        recv_sem=recv,
        device_id=peer,
        device_id_type=MESH,
    )


def pre_kernel(
    rows, cols, x_ref, gain_ref, cot_ref,
    xin_ref, call_ref, avg_ref, factor_ref,
    mine, stats, stat_send, stat_recv, row_send, row_recv,
):
    dp, row, col = lax.axis_index("dp"), lax.axis_index("row"), lax.axis_index("col")
    images, patches, width = x_ref.shape
    tokens = images * patches

    def col_peer(k):
        return (dp, row, lax.rem(col + k, cols))

    def row_peer(k):
        return (dp, lax.rem(row + k, rows), col)

    greet([col_peer(k) for k in range(1, cols)] + [row_peer(k) for k in range(1, rows)])
    here = pl.ds(pl.multiple_of(row * patches, patches), patches)
    sends = []
    for k in range(1, rows):
        copy = remote(
            cot_ref, call_ref.at[:, here, :], row_send.at[0, k - 1], row_recv.at[0, k - 1], row_peer(k)
        )
        copy.start()
        sends.append(copy)
    x = x_ref[...].astype(F32).reshape(tokens, width)
    ones = jnp.ones((8, width), F32)
    first = exact_nt(ones, x)
    second = exact_nt(ones, x * x)
    which = lax.broadcasted_iota(jnp.int32, (8, tokens), 0)
    local = jnp.where(which == 0, first, second)
    mine[...] = local
    stat_copies = []
    for k in range(1, cols):
        copy = remote(mine, stats.at[k - 1], stat_send.at[k - 1], stat_recv.at[k - 1], col_peer(k))
        copy.start()
        stat_copies.append(copy)
    call_ref[:, here, :] = cot_ref[...]
    total = local
    for k in range(1, cols):
        stat_copies[k - 1].wait_recv()
        total = total + stats[k - 1]
    total = total * (1.0 / (width * cols))
    average = total[0:1]
    factor = lax.rsqrt(total[1:2] - average * average + EPS)
    both = jnp.where(which == 0, average, factor)
    eye = (
        lax.broadcasted_iota(jnp.int32, (tokens, tokens), 0)
        == lax.broadcasted_iota(jnp.int32, (tokens, tokens), 1)
    ).astype(F32)
    turned = exact_nt(eye, both)
    avg_col, factor_col = turned[:, 0:1], turned[:, 1:2]
    normed = (x - avg_col) * factor_col
    xin_ref[:, here, :] = (normed * gain_ref[...]).astype(BF16).reshape(images, patches, width)
    for k in range(1, rows):
        copy = remote(
            xin_ref.at[:, here, :],
            xin_ref.at[:, here, :],
            row_send.at[1, k - 1],
            row_recv.at[1, k - 1],
            row_peer(k),
        )
        copy.start()
        sends.append(copy)
    avg_ref[...] = jnp.broadcast_to(avg_col, avg_ref.shape)
    factor_ref[...] = jnp.broadcast_to(factor_col, factor_ref.shape)
    for copy in sends:
        copy.wait_recv()
    for copy in sends + stat_copies:
        copy.wait_send()


def vmem(count):
    return [pl.BlockSpec(memory_space=pltpu.VMEM)] * count


def gather_inputs(features, ln_gain, cotangent):
    rows, cols = lax.axis_size("row"), lax.axis_size("col")
    images, patches, width = features.shape
    tokens = images * patches
    whole = jax.ShapeDtypeStruct((images, patches * rows, width), BF16)
    column = jax.ShapeDtypeStruct((tokens, HEAD), F32)
    return pl.pallas_call(
        functools.partial(pre_kernel, rows, cols),
        out_shape=(whole, whole, column, column),
        in_specs=vmem(3),
        out_specs=tuple(vmem(4)),
        scratch_shapes=[
            pltpu.VMEM((8, tokens), F32),
            pltpu.VMEM((cols - 1, 8, tokens), F32),
            pltpu.SemaphoreType.DMA((cols - 1,)),
            pltpu.SemaphoreType.DMA((cols - 1,)),
            pltpu.SemaphoreType.DMA((2, max(rows - 1, 1))),
            pltpu.SemaphoreType.DMA((2, max(rows - 1, 1))),
        ],
        compiler_params=pltpu.CompilerParams(collective_id=0, has_side_effects=True),
        name="gather_inputs",
    )(features, ln_gain.reshape(1, width), cotangent)


def owner_z(piece):
    return piece if piece < 3 else piece - 3 if piece < 6 else 3


def owner_slot(piece):
    return 0 if piece < 3 else 1 if piece < 6 else piece - 6


UNITS = 20
STEPS = PIECES + 3


def core_kernel(
    dps, rows, cols,
    x_ref, c_ref, wq_ref, wup_ref, wout_ref, wdown_ref, gain_ref,
    feat_ref, cot_ref, ln_ref, avg_ref, factor_ref,
    output_ref, input_grad_ref, ln_grad_ref, gains_ref, qkv_ref, up_ref, out_ref, down_ref,
    g_ref, opp, right_send, left_send, right_acc, left_acc, own,
    half_left, half_right, full_left, full_right, z_send, z_recv,
    dhalf_left, dhalf_right, dfull_left, dfull_right,
    x_turned, c_turned, out_acc, norm_acc, row_out, row_in,
    gain_mine, gain_in, stat_mine, stat_in, last_mine, last_in,
    s_opp, r_half, s_side, r_full, s_z, r_z, s_own, r_own, s_fwd, r_fwd, s_zag, r_zag,
    s_dopp, r_dhalf, s_dside, r_dfull, s_row, r_row, s_gain, r_gain, s_stat, r_stat, s_last, r_last,
):
    dp, row, col = lax.axis_index("dp"), lax.axis_index("row"), lax.axis_index("col")
    xi, zi = col // SIDE, lax.rem(col, SIDE)
    xr, xl, xo = lax.rem(xi + 1, SIDE), lax.rem(xi + 3, SIDE), lax.rem(xi + 2, SIDE)
    right, left = (dp, row, xr * SIDE + zi), (dp, row, xl * SIDE + zi)
    images, patches, width = x_ref.shape
    own_patches = patches // rows
    tokens = images * own_patches
    teams = dps * rows
    full_rows, half_rows = 4 * patches, 2 * patches

    def z_peer(k):
        return (dp, row, xi * SIDE + lax.rem(zi + k, SIDE))

    def col_peer(k):
        return (dp, row, lax.rem(col + k, cols))

    def row_peer(k):
        return (dp, lax.rem(row + k, rows), col)

    def team_peer(k):
        other = lax.rem(dp * rows + row + k, teams)
        return (other // rows, lax.rem(other, rows), col)

    greet([col_peer(k) for k in range(1, cols)] + [team_peer(k) for k in range(1, teams)])

    def run_start(block, pair):
        dest = lax.rem(block + pair, 4)
        return (dest * 6 + pair * 2) * HEAD, dest

    def partial_block(block, emit):
        image, run = block // 2, lax.rem(block, 2)
        triple = pl.ds(pl.multiple_of(run * 3 * HEAD, 3 * HEAD), 3 * HEAD)
        for part in range(3):
            start = part * 6 * HEAD + run * 3 * HEAD
            values = dot(x_ref[image], wq_ref[:, pl.ds(pl.multiple_of(start, HEAD), 3 * HEAD)])
            for z in range(3):
                emit(z, part, values[:, z * HEAD : (z + 1) * HEAD])
        values = dot_nt(c_ref[image], wout_ref[triple, :])
        for z in range(3):
            emit(z, 3, values[:, z * HEAD : (z + 1) * HEAD])
        for pair in range(3):
            start, _ = run_start(block, pair)
            hidden = pl.ds(pl.multiple_of(start, 2 * HEAD), 2 * HEAD)
            for im in range(2):
                values = dot(x_ref[im], wup_ref[:, hidden])
                for j in range(2):
                    emit(3 + 2 * pair + j, im, values[:, j * HEAD : (j + 1) * HEAD])
                values = dot_nt(c_ref[im], wdown_ref[hidden, :])
                for j in range(2):
                    emit(3 + 2 * pair + j, 2 + im, values[:, j * HEAD : (j + 1) * HEAD])

    def at(ref, p, part, parts=1):
        return ref.at[span(p, part, parts)]

    def span(p, part, parts=1):
        return pl.ds(pl.multiple_of(p * full_rows + part * patches, patches), parts * patches)

    def half_span(p):
        return pl.ds(pl.multiple_of(p * half_rows, half_rows), half_rows)

    def opp_right(p):
        return remote(
            at(opp, p, 0, 2), half_left.at[half_span(p)], s_opp.at[0, p], r_half.at[0, p], right
        )

    def opp_left(p):
        return remote(
            at(opp, p, 2, 2), half_right.at[half_span(p)], s_opp.at[1, p], r_half.at[1, p], left
        )

    def side_right(p, half):
        return remote(
            at(right_send, p, 2 * half, 2),
            at(full_left, p, 2 * half, 2),
            s_side.at[0, half, p],
            r_full.at[0, half, p],
            right,
        )

    def side_left(p, half):
        return remote(
            at(left_send, p, 2 * half, 2),
            at(full_right, p, 2 * half, 2),
            s_side.at[1, half, p],
            r_full.at[1, half, p],
            left,
        )

    def turn_order(i):
        return lax.rem(i + 2, 3) * 3 + i // 3

    def emit_opp(p, part, values):
        opp[span(p, part)] = values.astype(BF16)

    partial_block(xo, emit_opp)

    def send_opp(i, carry):
        p = turn_order(i)
        opp_right(p).start()
        opp_left(p).start()
        return carry

    lax.fori_loop(0, PIECES, send_opp, 0)

    def emit_right(p, part, values):
        if part >= 2:
            right_send[span(p, part)] = values.astype(BF16)
        else:
            right_acc[pl.ds(p * half_rows + part * patches, patches)] = values

    partial_block(xr, emit_right)

    def emit_left(p, part, values):
        if part < 2:
            left_send[span(p, part)] = values.astype(BF16)
        else:
            left_acc[pl.ds(p * half_rows + (part - 2) * patches, patches)] = values

    partial_block(xl, emit_left)

    def pass_on(i, carry):
        p = turn_order(i)
        side_right(p, 1).start()
        side_left(p, 0).start()
        opp_right(p).wait_recv()
        right_send[span(p, 0, 2)] = (
            right_acc[half_span(p)] + half_left[half_span(p)].astype(F32)
        ).astype(BF16)
        side_right(p, 0).start()
        opp_left(p).wait_recv()
        left_send[span(p, 2, 2)] = (
            left_acc[half_span(p)] + half_right[half_span(p)].astype(F32)
        ).astype(BF16)
        side_left(p, 1).start()
        return carry

    lax.fori_loop(0, PIECES, pass_on, 0)

    def emit_own(p, part, values):
        own[span(p, part)] = values

    partial_block(xi, emit_own)
    for im in range(images):
        here = slice(im * patches, (im + 1) * patches)
        x_turned[:, here] = x_ref[im].T
        c_turned[:, here] = c_ref[im].T

    def z_copy(p, k):
        return remote(
            at(z_send, p, 0, 4),
            z_recv.at[k - 1, owner_slot(p)],
            s_z.at[p],
            r_z.at[k - 1, owner_slot(p)],
            z_peer(k),
        )

    for i in range(PIECES):
        p = ((i + 2) % 3) * 3 + i // 3
        for half in range(2):
            side_right(p, half).wait_recv()
            side_left(p, half).wait_recv()
        here = span(p, 0, 4)
        own[here] = own[here] + full_left[here].astype(F32) + full_right[here].astype(F32)
        for k in range(1, SIDE):

            @pl.when(lax.rem(zi + k, SIDE) == owner_z(p))
            def _():
                z_send[here] = own[here].astype(BF16)
                z_copy(p, k).start()

    def arrived(p, slot):
        for k in range(1, SIDE):
            remote(
                at(z_send, 0, 0, 4),
                z_recv.at[k - 1, slot],
                s_z.at[0],
                r_z.at[k - 1, slot],
                z_peer(k),
            ).wait_recv()

    def summed(p, slot, part):
        total = own[span(p, part)]
        here = slice(part * patches, (part + 1) * patches)
        for k in range(1, SIDE):
            total = total + z_recv[k - 1, slot, here].astype(F32)
        return total

    def own_ag(p, way):
        peer = right if way == 0 else left
        return remote(g_ref.at[xi, p], g_ref.at[xi, p], s_own.at[way, p], r_own.at[way, p], peer)

    def z_ag(p, k):
        return remote(g_ref.at[xi, p], g_ref.at[xi, p], s_zag.at[k - 1, p], r_zag.at[p], z_peer(k))

    def launch(p):
        for way in range(2):
            own_ag(p, way).start()
        for k in range(1, SIDE):
            z_ag(p, k).start()

    def hidden_units(p, slot):
        arrived(p, slot)
        for im in range(2):
            value, slope = gelu_both(summed(p, slot, im))
            g_ref[xi, p, im] = value.astype(BF16)
            g_ref[xi, p, 2 + im] = (summed(p, slot, 2 + im) * slope).astype(BF16)
        launch(p)

    scale = HEAD ** (-0.5)

    def attention(p):
        arrived(p, 0)
        query_hat, query_factor = normalize(summed(p, 0, 0))
        key_hat, key_factor = normalize(summed(p, 0, 1))
        query_gain, key_gain = gain_ref[0:1, :], gain_ref[1:2, :]
        query = (query_hat * query_gain).astype(BF16)
        key = (key_hat * key_gain).astype(BF16)
        value = summed(p, 0, 2).astype(BF16)
        grad = summed(p, 0, 3).astype(BF16)
        expo = jnp.exp(dot_nt(query, key) * scale)
        weights = expo / jnp.sum(expo, -1, keepdims=True)
        weights_half = weights.astype(BF16)
        g_ref[xi, p, 0] = dot(weights_half, value).astype(BF16)
        weight_grad = dot_nt(grad, value)
        score_grad = weights * (weight_grad - jnp.sum(weights * weight_grad, -1, keepdims=True))
        score_grad = score_grad.astype(BF16)
        query_grad = dot(score_grad, key) * scale
        key_grad = dot(score_grad.T, query) * scale
        value_grad = dot(weights_half.T, grad)
        gain_mine[0:1, :] = jnp.sum(query_grad * query_hat, 0, keepdims=True)
        gain_mine[1:2, :] = jnp.sum(key_grad * key_hat, 0, keepdims=True)
        g_ref[xi, p, 1] = norm_back(query_grad, query_hat, query_factor, query_gain).astype(BF16)
        g_ref[xi, p, 2] = norm_back(key_grad, key_hat, key_factor, key_gain).astype(BF16)
        g_ref[xi, p, 3] = value_grad.astype(BF16)
        launch(p)

    gain_mine[...] = jnp.zeros_like(gain_mine)

    @pl.when(zi < 3)
    def _():
        hidden_units(zi + 3, 1)
        attention(zi)

    @pl.when(zi == 3)
    def _():
        for j in range(3):
            hidden_units(6 + j, j)

    def gain_copy(k):
        return remote(
            gain_mine, gain_in.at[k - 1], s_gain.at[k - 1], r_gain.at[k - 1], col_peer(k)
        )

    for k in range(1, cols):
        gain_copy(k).start()

    def settle(p, carry):
        opp_right(p).wait_send()
        opp_left(p).wait_send()
        for half in range(2):
            side_right(p, half).wait_send()
            side_left(p, half).wait_send()
        return carry

    lax.fori_loop(0, PIECES, settle, 0)
    out_acc[...] = jnp.zeros_like(out_acc)
    norm_acc[...] = jnp.zeros_like(norm_acc)

    low, high = pl.ds(0, 2), pl.ds(2, 2)

    def fwd_copy(p, way):
        block = xl if way == 0 else xr
        part = low if way == 0 else high
        there = right if way == 0 else left
        return remote(
            g_ref.at[block, p, part],
            g_ref.at[block, p, part],
            s_fwd.at[way, p],
            r_fwd.at[way, p],
            there,
        )

    own_count = jnp.where(zi == 3, 3, 2)

    def piece_at(i):
        piece, start = i * 0, 0
        for step in range(SIDE):
            z = lax.rem(zi + step, SIDE)
            count = jnp.where(z == 3, 3, 2)
            slot = i - start
            named = jnp.where(z == 3, 6 + slot, z + 3 * slot)
            piece = jnp.where((slot >= 0) & (slot < count), named, piece)
            start = start + count
        return piece

    dp_right = (lax.rem(dp + 1, dps), row, col)
    dp_left = (lax.rem(dp + dps - 1, dps), row, col)
    half_width = width // 2

    def unit_span(u, half=None):
        if half is None:
            return pl.ds(pl.multiple_of(u * width, width), width)
        return pl.ds(pl.multiple_of(u * width + half * half_width, half_width), half_width)

    def small_span(u):
        return pl.ds(pl.multiple_of(u * half_width, half_width), half_width)

    def dopp_right(u):
        return remote(
            opp.at[unit_span(u, 0)], dhalf_left.at[small_span(u)],
            s_dopp.at[0, u], r_dhalf.at[0, u], dp_right,
        )

    def dopp_left(u):
        return remote(
            opp.at[unit_span(u, 1)], dhalf_right.at[small_span(u)],
            s_dopp.at[1, u], r_dhalf.at[1, u], dp_left,
        )

    def dside_right(u, half):
        return remote(
            right_send.at[unit_span(u, half)], dfull_left.at[unit_span(u, half)],
            s_dside.at[0, half, u], r_dfull.at[0, half, u], dp_right,
        )

    def dside_left(u, half):
        return remote(
            left_send.at[unit_span(u, half)], dfull_right.at[unit_span(u, half)],
            s_dside.at[1, half, u], r_dfull.at[1, half, u], dp_left,
        )

    def emit_unit(dest, u, values):
        away = lax.rem(dest - dp + 4, 4)

        @pl.when(away == 0)
        def _():
            own[unit_span(u)] = values

        if dps == 1:
            return

        @pl.when(away == 2)
        def _():
            opp[unit_span(u)] = values.astype(BF16)
            dopp_right(u).start()
            dopp_left(u).start()

        @pl.when(away == 1)
        def _():
            right_acc[small_span(u)] = values[:half_width]
            right_send[unit_span(u, 1)] = values[half_width:].astype(BF16)
            dside_right(u, 1).start()

        @pl.when(away == 3)
        def _():
            left_acc[small_span(u)] = values[half_width:]
            left_send[unit_span(u, 0)] = values[:half_width].astype(BF16)
            dside_left(u, 0).start()

    def pass_unit(dest, u):
        if dps == 1:
            return
        away = lax.rem(dest - dp + 4, 4)

        @pl.when(away == 1)
        def _():
            dopp_right(u).wait_recv()
            right_send[unit_span(u, 0)] = (
                right_acc[small_span(u)] + dhalf_left[small_span(u)].astype(F32)
            ).astype(BF16)
            dside_right(u, 0).start()

        @pl.when(away == 3)
        def _():
            dopp_left(u).wait_recv()
            left_send[unit_span(u, 1)] = (
                left_acc[small_span(u)] + dhalf_right[small_span(u)].astype(F32)
            ).astype(BF16)
            dside_left(u, 1).start()

    def hidden_place(block, p):
        pair, second = (p - 3) // 2, lax.rem(p - 3, 2)
        start, dest = run_start(block, pair)
        return pl.multiple_of(start + second * HEAD, HEAD), dest, pair * 2 + second

    def hidden_back(block, p):
        start, dest, u = hidden_place(block, p)
        run = pl.ds(start, HEAD)
        hidden = g_ref[block, p, low].reshape(half_rows, HEAD)
        pre = g_ref[block, p, high].reshape(half_rows, HEAD)
        emit_unit(dest, u, dot(x_turned[...], pre))
        emit_unit(dest, 6 + u, dot(c_turned[...], hidden))
        out_acc[...] += dot(hidden, wdown_ref[run, :])
        norm_acc[...] += dot_nt(pre, wup_ref[:, run])

    def attention_dests(run, z):
        return 2 * run + jnp.where(z == 2, 1, 0), 2 * run + 1, jnp.where(z == 1, 1, 0)

    def attention_back(block, z):
        image, run = block // 2, lax.rem(block, 2)
        head = run * 3 + z
        here = pl.ds(pl.multiple_of(image * patches, patches), patches)
        out_acc[here] += dot(
            g_ref[block, z, 0], wout_ref[pl.ds(pl.multiple_of(head * HEAD, HEAD), HEAD), :]
        )
        total = norm_acc[here]
        for part in range(3):
            columns = pl.ds(pl.multiple_of((part * 6 + head) * HEAD, HEAD), HEAD)
            total = total + dot_nt(g_ref[block, z, 1 + part], wq_ref[:, columns])
        norm_acc[here] = total

    def attention_weights(run, z):
        dest, second, which = attention_dests(run, z)
        for t in range(4):
            turned = c_turned if t == 3 else x_turned
            part = 0 if t == 3 else t + 1
            values = dot(turned[:, 0:patches], g_ref[run, z, part]) + dot(
                turned[:, patches : 2 * patches], g_ref[run + 2, z, part]
            )
            u = 12 + 2 * t + which
            emit_unit(dest, u, values)

            @pl.when(z == 1)
            def _():
                emit_unit(second, u, values)

    def pass_hidden(block, p):
        _, dest, u = hidden_place(block, p)
        pass_unit(dest, u)
        pass_unit(dest, 6 + u)

    def pass_attention(run, z):
        dest, second, which = attention_dests(run, z)
        for t in range(4):
            u = 12 + 2 * t + which
            pass_unit(dest, u)

            @pl.when(z == 1)
            def _():
                pass_unit(second, u)

    def step(i, carry):
        ahead = i + 2

        @pl.when((ahead >= own_count) & (ahead < PIECES))
        def _():
            p = piece_at(ahead)
            z_ag(p, 1).wait_recv()
            for way in range(2):
                own_ag(p, way).start()

        @pl.when(i < PIECES)
        def _():
            p = piece_at(i)
            for way in range(2):
                own_ag(p, way).wait_recv()
                fwd_copy(p, way).start()

        @pl.when((i >= 2) & (i < PIECES + 2))
        def _():
            p = piece_at(i - 2)
            for way in range(2):
                fwd_copy(p, way).wait_recv()

        def each_block(k, carry):
            block = lax.rem(xi + k, 4)
            turn = i - jnp.where(k == 2, 2, 0)
            p = piece_at(turn)
            live = (turn >= 0) & (turn < PIECES)

            @pl.when(live & (p >= 3))
            def _():
                hidden_back(block, p)

            @pl.when(live & (p < 3))
            def _():
                attention_back(block, p)

            @pl.when(live & (p < 3) & (k >= 2))
            def _():
                attention_weights(lax.rem(block, 2), p)

            return carry

        lax.fori_loop(0, SIDE, each_block, 0)

        def each_pass(k, carry):
            block = lax.rem(xi + k, 4)
            turn = i - jnp.where(k == 2, 3, 1)
            p = piece_at(turn)
            live = (turn >= 0) & (turn < PIECES)

            @pl.when(live & (p >= 3))
            def _():
                pass_hidden(block, p)

            @pl.when(live & (p < 3) & (k >= 2))
            def _():
                pass_attention(lax.rem(block, 2), p)

            return carry

        lax.fori_loop(0, SIDE, each_pass, 0)
        return carry

    lax.fori_loop(0, STEPS, step, 0)

    for which, acc in enumerate((out_acc, norm_acc)):
        for im in range(images):
            here = slice(im * patches, (im + 1) * patches)
            row_out[which, im] = acc[here].astype(BF16)

    def row_copy(k):
        there = lax.rem(row + k, rows)
        return remote(
            row_out.at[:, :, pl.ds(pl.multiple_of(there * own_patches, own_patches), own_patches), :],
            row_in.at[k - 1],
            s_row.at[k - 1],
            r_row.at[k - 1],
            row_peer(k),
        )

    for k in range(1, rows):
        row_copy(k).start()
    for k in range(1, rows):
        row_copy(k).wait_recv()

    def row_total(which, acc):
        parts = []
        for im in range(images):
            start = im * patches + row * own_patches
            total = acc[pl.ds(pl.multiple_of(start, own_patches), own_patches)]
            for k in range(1, rows):
                total = total + row_in[k - 1, which, im].astype(F32)
            parts.append(total)
        return jnp.concatenate(parts, 0)

    inputs_wide = feat_ref[...].astype(F32).reshape(tokens, width)
    average, factor = avg_ref[:, 0:1], factor_ref[:, 0:1]
    normed = (inputs_wide - average) * factor
    norm_grad = row_total(1, norm_acc)
    scaled = norm_grad * ln_ref[...]
    ones = jnp.ones((8, width), F32)
    which = lax.broadcasted_iota(jnp.int32, (8, tokens), 0)
    stats = jnp.where(which == 0, exact_nt(ones, scaled), exact_nt(ones, scaled * normed))
    stat_mine[...] = stats

    def stat_copy(k):
        return remote(
            stat_mine, stat_in.at[k - 1], s_stat.at[k - 1], r_stat.at[k - 1], col_peer(k)
        )

    for k in range(1, cols):
        stat_copy(k).start()
    gains = gain_mine[...]
    for k in range(1, cols):
        gain_copy(k).wait_recv()
        gains = gains + gain_in[k - 1]
    last_mine[:, 0:HEAD] = gains
    last_mine[:, HEAD:] = jnp.broadcast_to(
        jnp.sum(norm_grad * normed, 0, keepdims=True), (8, width)
    )

    def last_copy(k):
        return remote(
            last_mine, last_in.at[k - 1], s_last.at[k - 1], r_last.at[k - 1], team_peer(k)
        )

    for k in range(1, teams):
        last_copy(k).start()
    output_ref[...] = (
        (inputs_wide + row_total(0, out_acc)).astype(BF16).reshape(images, own_patches, width)
    )
    for k in range(1, cols):
        stat_copy(k).wait_recv()
        stats = stats + stat_in[k - 1]
    stats = stats * (1.0 / (width * cols))
    eye = (
        lax.broadcasted_iota(jnp.int32, (tokens, tokens), 0)
        == lax.broadcasted_iota(jnp.int32, (tokens, tokens), 1)
    ).astype(F32)
    turned = exact_nt(eye, stats)
    centre, along = turned[:, 0:1], turned[:, 1:2]
    input_grad = cot_ref[...].astype(F32).reshape(tokens, width) + factor * (
        scaled - centre - normed * along
    )
    input_grad_ref[...] = input_grad.astype(BF16).reshape(images, own_patches, width)

    def unit_total(u):
        here = unit_span(u)
        total = own[here]
        if dps > 1:
            for half in range(2):
                dside_right(u, half).wait_recv()
                dside_left(u, half).wait_recv()
            total = total + dfull_left[here].astype(F32) + dfull_right[here].astype(F32)
        return total

    for u in range(6):
        columns = slice(u * HEAD, (u + 1) * HEAD)
        up_ref[:, columns] = unit_total(u)
        down_ref[columns, :] = unit_total(6 + u).T
        qkv_ref[u] = unit_total(12 + u)
    whole, split = unit_total(18).T, unit_total(19).T
    mid = HEAD // 2

    @pl.when(lax.rem(dp, 2) == 0)
    def _():
        out_ref[0:HEAD, :] = whole
        out_ref[HEAD : HEAD + mid, :] = split[0:mid]

    @pl.when(lax.rem(dp, 2) == 1)
    def _():
        out_ref[0:mid, :] = split[mid:]
        out_ref[mid : HEAD + mid, :] = whole

    last = last_mine[...]
    for k in range(1, teams):
        last_copy(k).wait_recv()
        last = last + last_in[k - 1]
    gains_ref[...] = last[:, 0:HEAD]
    ln_grad_ref[...] = last[0:1, HEAD:]

    def finish(p, carry):
        for way in range(2):
            own_ag(p, way).wait_send()
            fwd_copy(p, way).wait_send()
        return carry

    lax.fori_loop(0, PIECES, finish, 0)

    def finish_unit(u, carry):
        dopp_right(u).wait_send()
        dopp_left(u).wait_send()
        for half in range(2):
            dside_right(u, half).wait_send()
            dside_left(u, half).wait_send()
        return carry

    if dps > 1:
        lax.fori_loop(0, UNITS, finish_unit, 0)
    for p in range(PIECES):

        @pl.when(zi != owner_z(p))
        def _():
            z_copy(p, 1).wait_send()

        @pl.when(zi == owner_z(p))
        def _():
            for k in range(1, SIDE):
                z_ag(p, k).wait_send()

    for k in range(1, cols):
        gain_copy(k).wait_send()
        stat_copy(k).wait_send()
    for k in range(1, rows):
        row_copy(k).wait_send()
    for k in range(1, teams):
        last_copy(k).wait_send()


def exchange(
    x_all, c_all, w_qkv, w_up, w_out, w_down, qk_gain, features, cotangent, ln_gain, average, factor
):
    dps, rows, cols = lax.axis_size("dp"), lax.axis_size("row"), lax.axis_size("col")
    images, patches, width = x_all.shape
    own_patches = features.shape[1]
    tokens = images * own_patches
    teams = dps * rows
    dma = pltpu.SemaphoreType.DMA
    whole = max(PIECES * 4 * patches, UNITS * width)
    half = max(PIECES * 2 * patches, UNITS * width // 2)
    units = UNITS * width
    struct = jax.ShapeDtypeStruct
    others, mates, peers = max(teams - 1, 1), max(rows - 1, 1), cols - 1
    return pl.pallas_call(
        functools.partial(core_kernel, dps, rows, cols),
        out_shape=(
            struct(features.shape, BF16),
            struct(features.shape, BF16),
            struct((1, width), F32),
            struct((8, HEAD), F32),
            struct((6, width, HEAD), F32),
            struct((width, 6 * HEAD), F32),
            struct((3 * HEAD // 2, width), F32),
            struct((6 * HEAD, width), F32),
        ),
        in_specs=vmem(12),
        out_specs=tuple(vmem(8)),
        scratch_shapes=[
            pltpu.VMEM((SIDE, PIECES, 4, patches, HEAD), BF16),
            pltpu.VMEM((whole, HEAD), BF16),
            pltpu.VMEM((whole, HEAD), BF16),
            pltpu.VMEM((whole, HEAD), BF16),
            pltpu.VMEM((half, HEAD), F32),
            pltpu.VMEM((half, HEAD), F32),
            pltpu.VMEM((whole, HEAD), F32),
            pltpu.VMEM((PIECES * 2 * patches, HEAD), BF16),
            pltpu.VMEM((PIECES * 2 * patches, HEAD), BF16),
            pltpu.VMEM((PIECES * 4 * patches, HEAD), BF16),
            pltpu.VMEM((PIECES * 4 * patches, HEAD), BF16),
            pltpu.VMEM((PIECES * 4 * patches, HEAD), BF16),
            pltpu.VMEM((SIDE - 1, 3, 4 * patches, HEAD), BF16),
            pltpu.VMEM((units // 2, HEAD), BF16),
            pltpu.VMEM((units // 2, HEAD), BF16),
            pltpu.VMEM((units, HEAD), BF16),
            pltpu.VMEM((units, HEAD), BF16),
            pltpu.VMEM((width, images * patches), BF16),
            pltpu.VMEM((width, images * patches), BF16),
            pltpu.VMEM((images * patches, width), F32),
            pltpu.VMEM((images * patches, width), F32),
            pltpu.VMEM((2, images, patches, width), BF16),
            pltpu.VMEM((mates, 2, images, own_patches, width), BF16),
            pltpu.VMEM((8, HEAD), F32),
            pltpu.VMEM((peers, 8, HEAD), F32),
            pltpu.VMEM((8, tokens), F32),
            pltpu.VMEM((peers, 8, tokens), F32),
            pltpu.VMEM((8, HEAD + width), F32),
            pltpu.VMEM((others, 8, HEAD + width), F32),
            dma((2, PIECES)),
            dma((2, PIECES)),
            dma((2, 2, PIECES)),
            dma((2, 2, PIECES)),
            dma((PIECES,)),
            dma((SIDE - 1, 3)),
            dma((2, PIECES)),
            dma((2, PIECES)),
            dma((2, PIECES)),
            dma((2, PIECES)),
            dma((SIDE - 1, PIECES)),
            dma((PIECES,)),
            dma((2, UNITS)),
            dma((2, UNITS)),
            dma((2, 2, UNITS)),
            dma((2, 2, UNITS)),
            dma((mates,)),
            dma((mates,)),
            dma((peers,)),
            dma((peers,)),
            dma((peers,)),
            dma((peers,)),
            dma((others,)),
            dma((others,)),
        ],
        compiler_params=pltpu.CompilerParams(
            collective_id=1, has_side_effects=True, vmem_limit_bytes=VMEM_BYTES
        ),
        name="exchange",
    )(
        x_all, c_all, w_qkv, w_up, w_out, w_down, qk_gain,
        features, cotangent, ln_gain, average, factor,
    )


def on_device(features, ln_gain, w_qkv, qk_gain, w_up, w_out, w_down, cotangent):
    images, patches, width = features.shape
    head_cols = w_qkv.shape[2]
    x_all, c_all, average, factor = gather_inputs(features, ln_gain, cotangent)
    qkv_flat = w_qkv.reshape(width, 3 * head_cols)
    output, input_grad, ln_grad, gains, qkv_units, up_grad, out_grad, down_grad = exchange(
        x_all, c_all, qkv_flat, w_up, w_out, w_down, qk_gain,
        features, cotangent, ln_gain.reshape(1, width), average, factor,
    )
    units = qkv_units.reshape(3, 2, width, HEAD)
    whole, split = units[:, 0], units[:, 1]
    mid = HEAD // 2
    qkv_grad = jnp.where(
        lax.rem(lax.axis_index("dp"), 2) == 0,
        jnp.concatenate([whole, split[..., :mid]], -1),
        jnp.concatenate([split[..., mid:], whole], -1),
    )
    qkv_grad = jnp.transpose(qkv_grad, (1, 0, 2))
    return (
        output, input_grad, ln_grad.reshape(width), gains[:2], qkv_grad, up_grad, out_grad, down_grad
    )


def solution(mesh):
    in_specs = (
        P("dp", "row", "col"),
        P("col"),
        P("col", None, "row"),
        P(),
        P("col", "row"),
        P("row", "col"),
        P("row", "col"),
        P("dp", "row", "col"),
    )
    out_specs = (
        P("dp", "row", "col"),
        P("dp", "row", "col"),
        P("col"),
        P(),
        P("col", None, ("row", "dp")),
        P("col", ("row", "dp")),
        P(("row", "dp"), "col"),
        P(("row", "dp"), "col"),
    )
    return jax.shard_map(
        on_device, mesh=mesh, in_specs=in_specs, out_specs=out_specs, check_vma=False
    )
```

time: 533 us -> 317 us (0.59)
  blocking collectives: 199 us -> 0 us
  Pallas kernels: 238 us -> 301 us
  local copies, waits for them, and re-layouts: 41.9 us -> 13.6 us
  matrix products: 26 us -> 0 us
  between operations: 14.3 us -> 0.72 us
  other arithmetic: 10.9 us -> 1.58 us
    psum x3 -> x0, blocking collectives: 199 us -> none  [the longest x1 114 us: on_device(): gain_grads = lax.psum(gains[:2], ('dp', 'row', 'col'))]
    pallas_call x1, Pallas kernels: 208 us -> 271 us  [exchange(): pl.pallas_call(functools.partial(core_kernel, dps, rows, cols), out_shape...]
    dot_general x8 -> x0, matrix products: 26 us -> none  [ein(): return jnp.einsum(spec, a, b, preferred_element_type=F32)]
    transpose x3 -> x0, local copies, waits for them, and re-layouts: 11.1 us -> none  [units_of(): jnp.transpose(values, (2, 3, 0, 1, 4))]
    convert_element_type x5 -> x0, other arithmetic: 9.78 us -> none  [the longest x4 7.95 us: dp_sum(): return lax.psum_scatter(values.astype(BF16), 'dp', scatter_dimension=dim,...]
    another operation x4 -> x0, local copies, waits for them, and re-layouts: 8.03 us -> none  [heads_of(): values = pieces[:, 0:3, part].reshape(2, 2, 3, every, HEAD)]
    reshape x3 -> x0, local copies, waits for them, and re-layouts: 6.88 us -> none  [heads_of(): jnp.transpose(values, (0, 3, 1, 2, 4)).reshape(images, every, head_cols)]
  transfers between devices with their start and end apart: 6 -> 0, of which waited for: 1 -> 0; matrix products, arithmetic and copies ran while one was open for 7% -> 0% of each run, Pallas kernels for 0% -> 0%
where the time goes in v2:
time: 317 us
  Pallas kernels  301 us (95%)
  local copies, waits for them, and re-layouts  13.6 us (4%)
    pallas_call x1, Pallas kernels, exchange(): pl.pallas_call(functools.partial(core_kernel, dps, rows, cols), out_shape...  271 us
    pallas_call x1, Pallas kernels, gather_inputs(): pl.pallas_call(functools.partial(pre_kernel, rows, cols), out_shape=(whol...  30.3 us
    unnamed x20, local copies, waits for them, and re-layouts  7.37 us

profile of v2, /device:TPU:1, one launch (start us, length us, event | category | flops | bytes accessed | tf_op | source)
XLA Modules:
  0.0 317.1 jit_solution(4310901983454694446)
XLA Ops:
  0.6 1.2 reshape.29.gain_ref.ln_ref
  1.9 30.3 %gather_inputs.1 = (bf16[2,256,384]{2,1,0:T(8,128)(2,1)}, bf16[2,256,384]{2,1,0:T(8,128)(2,1)}, f32[128,128]{1,0:T(8,128)}, f32[128,128]{1,0:T(8,128)}) custom-call(bf16[2,64,384]{2,1,0:T(8,128)(2,1)} %feat_ref.1, f32[1,384]{1,0:T(1,128)} %reshape.29.gain_ref.ln_ref, bf16[2,64,384]{2,1,0:T(8,128)(2,1)} %cot_ref.3), custom_call_target="tpu_custom_call" | custom-call | tf_op jit(solution)/shard_map/gather_inputs/pallas_call | solution.py:159
  32.2 2.8 copy.19
  34.9 2.4 copy.20.wq_ref
  37.3 271.0 %exchange.1 = (bf16[2,64,384]{2,1,0:T(8,128)(2,1)}, bf16[2,64,384]{2,1,0:T(8,128)(2,1)}, f32[1,384]{1,0:T(1,128)}, f32[8,128]{1,0:T(8,128)}, f32[6,384,128]{2,1,...) custom-call(bf16[2,256,384]{2,1,0:T(8,128)(2,1)} %get-tuple-element.20.x_ref, ...), custom_call_target="tpu_custom_call" | custom-call | tf_op jit(solution)/shard_map/exchange/pallas_call | solution.py:877
  308.2 1.3 fusion.1
  309.6 0.2 copy.24
  309.9 0.2 copy.23
  310.1 0.0 copy-start.5
  310.1 0.0 copy-start.4
  310.1 0.0 copy-start.3
  310.1 0.0 copy-start.1
  310.1 1.0 fusion
  311.1 0.0 copy-done.5
  311.1 0.6 reduce
  311.7 1.2 slice.15
  312.9 0.0 copy-done.4
  313.0 0.6 copy.30
  313.6 0.0 copy-done.3
  313.6 0.6 copy.31
  314.2 1.0 copy.32
  315.3 0.1 copy-done.2
  315.4 0.7 copy.33
  316.1 1.0 copy.34
  (5 shorter events, 0.0 us)
Async XLA Ops:
  310.1 1.0 copy-start.5
  310.1 2.9 copy-start.4
  310.1 3.5 %copy-start.3 = (bf16[2,64,384]{2,1,0:T(8,128)(2,1)S(1)}, bf16[2,64,384]{2,1,0:T(8,128)(2,1)}, u32[]{:S(2)}) copy-start(bf16[2,64,384]{2,1,0:T(8,128)(2,1)} %get-tuple-element.45) | copy-start | bytes 294916
  310.1 4.1 %copy-start.1 = (f32[384,768]{1,0:T(8,128)S(1)}, f32[384,768]{1,0:T(8,128)}, u32[]{:S(2)}) copy-start(f32[384,768]{1,0:T(8,128)} %get-tuple-element.49) | copy-start | bytes 3538948
  314.2 1.1 copy-start.2
  314.2 1.8 copy-start

commit v3 on v2

--- a/solution.py
+++ b/solution.py
@@ -75,105 +75,10 @@
     )
 
 
-def pre_kernel(
-    rows, cols, x_ref, gain_ref, cot_ref,
-    xin_ref, call_ref, avg_ref, factor_ref,
-    mine, stats, stat_send, stat_recv, row_send, row_recv,
-):
-    dp, row, col = lax.axis_index("dp"), lax.axis_index("row"), lax.axis_index("col")
-    images, patches, width = x_ref.shape
-    tokens = images * patches
-
-    def col_peer(k):
-        return (dp, row, lax.rem(col + k, cols))
-
-    def row_peer(k):
-        return (dp, lax.rem(row + k, rows), col)
-
-    greet([col_peer(k) for k in range(1, cols)] + [row_peer(k) for k in range(1, rows)])
-    here = pl.ds(pl.multiple_of(row * patches, patches), patches)
-    sends = []
-    for k in range(1, rows):
-        copy = remote(
-            cot_ref, call_ref.at[:, here, :], row_send.at[0, k - 1], row_recv.at[0, k - 1], row_peer(k)
-        )
-        copy.start()
-        sends.append(copy)
-    x = x_ref[...].astype(F32).reshape(tokens, width)
-    ones = jnp.ones((8, width), F32)
-    first = exact_nt(ones, x)
-    second = exact_nt(ones, x * x)
-    which = lax.broadcasted_iota(jnp.int32, (8, tokens), 0)
-    local = jnp.where(which == 0, first, second)
-    mine[...] = local
-    stat_copies = []
-    for k in range(1, cols):
-        copy = remote(mine, stats.at[k - 1], stat_send.at[k - 1], stat_recv.at[k - 1], col_peer(k))
-        copy.start()
-        stat_copies.append(copy)
-    call_ref[:, here, :] = cot_ref[...]
-    total = local
-    for k in range(1, cols):
-        stat_copies[k - 1].wait_recv()
-        total = total + stats[k - 1]
-    total = total * (1.0 / (width * cols))
-    average = total[0:1]
-    factor = lax.rsqrt(total[1:2] - average * average + EPS)
-    both = jnp.where(which == 0, average, factor)
-    eye = (
-        lax.broadcasted_iota(jnp.int32, (tokens, tokens), 0)
-        == lax.broadcasted_iota(jnp.int32, (tokens, tokens), 1)
-    ).astype(F32)
-    turned = exact_nt(eye, both)
-    avg_col, factor_col = turned[:, 0:1], turned[:, 1:2]
-    normed = (x - avg_col) * factor_col
-    xin_ref[:, here, :] = (normed * gain_ref[...]).astype(BF16).reshape(images, patches, width)
-    for k in range(1, rows):
-        copy = remote(
-            xin_ref.at[:, here, :],
-            xin_ref.at[:, here, :],
-            row_send.at[1, k - 1],
-            row_recv.at[1, k - 1],
-            row_peer(k),
-        )
-        copy.start()
-        sends.append(copy)
-    avg_ref[...] = jnp.broadcast_to(avg_col, avg_ref.shape)
-    factor_ref[...] = jnp.broadcast_to(factor_col, factor_ref.shape)
-    for copy in sends:
-        copy.wait_recv()
-    for copy in sends + stat_copies:
-        copy.wait_send()
-
-
 def vmem(count):
     return [pl.BlockSpec(memory_space=pltpu.VMEM)] * count
 
 
-def gather_inputs(features, ln_gain, cotangent):
-    rows, cols = lax.axis_size("row"), lax.axis_size("col")
-    images, patches, width = features.shape
-    tokens = images * patches
-    whole = jax.ShapeDtypeStruct((images, patches * rows, width), BF16)
-    column = jax.ShapeDtypeStruct((tokens, HEAD), F32)
-    return pl.pallas_call(
-        functools.partial(pre_kernel, rows, cols),
-        out_shape=(whole, whole, column, column),
-        in_specs=vmem(3),
-        out_specs=tuple(vmem(4)),
-        scratch_shapes=[
-            pltpu.VMEM((8, tokens), F32),
-            pltpu.VMEM((cols - 1, 8, tokens), F32),
-            pltpu.SemaphoreType.DMA((cols - 1,)),
-            pltpu.SemaphoreType.DMA((cols - 1,)),
-            pltpu.SemaphoreType.DMA((2, max(rows - 1, 1))),
-            pltpu.SemaphoreType.DMA((2, max(rows - 1, 1))),
-        ],
-        compiler_params=pltpu.CompilerParams(collective_id=0, has_side_effects=True),
-        name="gather_inputs",
-    )(features, ln_gain.reshape(1, width), cotangent)
-
-
 def owner_z(piece):
     return piece if piece < 3 else piece - 3 if piece < 6 else 3
 
@@ -183,20 +88,31 @@
 
 
 UNITS = 20
-STEPS = PIECES + 3
+BEHIND = 2
+LATE = 1
+STEPS = PIECES + 2 + LATE
+SUM_ORDER = (6, 0, 7, 3, 8, 1, 2, 4, 5)
+GATHER_ORDER = (
+    (0, 3, 1, 4, 2, 5, 6, 7, 8),
+    (1, 4, 0, 2, 3, 5, 6, 7, 8),
+    (2, 5, 1, 6, 4, 7, 0, 8, 3),
+    (6, 7, 8, 2, 5, 1, 4, 0, 3),
+)
 
 
 def core_kernel(
     dps, rows, cols,
-    x_ref, c_ref, wq_ref, wup_ref, wout_ref, wdown_ref, gain_ref,
-    feat_ref, cot_ref, ln_ref, avg_ref, factor_ref,
+    wq_hbm, wup_hbm, wout_hbm, wdown_hbm, gain_ref, feat_ref, cot_ref, ln_ref,
     output_ref, input_grad_ref, ln_grad_ref, gains_ref, qkv_ref, up_ref, out_ref, down_ref,
+    x_ref, c_ref, wq_ref, wup_ref, wout_ref, wdown_ref, avg_ref, factor_ref,
     g_ref, opp, right_send, left_send, right_acc, left_acc, own,
     half_left, half_right, full_left, full_right, z_send, z_recv,
     dhalf_left, dhalf_right, dfull_left, dfull_right,
-    x_turned, c_turned, out_acc, norm_acc, row_out, row_in,
+    x_turned, c_turned, out_acc, norm_acc, core_out, core_in, row_out, row_in,
+    norm_mine, norm_in,
     gain_mine, gain_in, stat_mine, stat_in, last_mine, last_in,
     s_opp, r_half, s_side, r_full, s_z, r_z, s_own, r_own, s_fwd, r_fwd, s_zag, r_zag,
+    s_load, s_norm, r_norm, s_rowg, r_rowg, s_core, r_core,
     s_dopp, r_dhalf, s_dside, r_dfull, s_row, r_row, s_gain, r_gain, s_stat, r_stat, s_last, r_last,
 ):
     dp, row, col = lax.axis_index("dp"), lax.axis_index("row"), lax.axis_index("col")
@@ -209,36 +125,97 @@
     teams = dps * rows
     full_rows, half_rows = 4 * patches, 2 * patches
 
-    def z_peer(k):
-        return (dp, row, xi * SIDE + lax.rem(zi + k, SIDE))
-
     def col_peer(k):
         return (dp, row, lax.rem(col + k, cols))
 
-    def row_peer(k):
-        return (dp, lax.rem(row + k, rows), col)
+    mate = (dp, row + 1 - 2 * lax.rem(row, 2), col)
+    cross = (dp, lax.rem(row + 2, rows), col)
 
     def team_peer(k):
         other = lax.rem(dp * rows + row + k, teams)
         return (other // rows, lax.rem(other, rows), col)
 
+    loads = [
+        pltpu.make_async_copy(src, dst, s_load.at[i])
+        for i, (src, dst) in enumerate(
+            ((wdown_hbm, wdown_ref), (wout_hbm, wout_ref), (wup_hbm, wup_ref), (wq_hbm, wq_ref))
+        )
+    ]
+    for load in loads:
+        load.start()
     greet([col_peer(k) for k in range(1, cols)] + [team_peer(k) for k in range(1, teams)])
+
+    def patch_rows(r):
+        return pl.ds(pl.multiple_of(r * own_patches, own_patches), own_patches)
+
+    def row_gather(which, ref, step):
+        here = ref.at[:, patch_rows(row if step < 2 else lax.rem(row + 2, rows)), :]
+        return remote(
+            here, here, s_rowg.at[which, step], r_rowg.at[which, step], cross if step == 1 else mate
+        )
+
+    def row_send(which, ref):
+        if rows > 1:
+            row_gather(which, ref, 1).start()
+            row_gather(which, ref, 0).start()
+
+    def row_arrive(which, ref):
+        if rows > 1:
+            row_gather(which, ref, 1).wait_recv()
+            row_gather(which, ref, 2).start()
+            row_gather(which, ref, 0).wait_recv()
+            row_gather(which, ref, 2).wait_recv()
+
+    c_ref[:, patch_rows(row), :] = cot_ref[...]
+    row_send(0, c_ref)
+    inputs_wide = feat_ref[...].astype(F32).reshape(tokens, width)
+    ones = jnp.ones((8, width), F32)
+    which = lax.broadcasted_iota(jnp.int32, (8, tokens), 0)
+    norm_sums = jnp.where(
+        which == 0, exact_nt(ones, inputs_wide), exact_nt(ones, inputs_wide * inputs_wide)
+    )
+    norm_mine[...] = norm_sums
+
+    def norm_copy(k):
+        return remote(
+            norm_mine, norm_in.at[k - 1], s_norm.at[k - 1], r_norm.at[k - 1], col_peer(k)
+        )
+
+    for k in range(1, cols):
+        norm_copy(k).start()
+    eye = (
+        lax.broadcasted_iota(jnp.int32, (tokens, tokens), 0)
+        == lax.broadcasted_iota(jnp.int32, (tokens, tokens), 1)
+    ).astype(F32)
 
     def run_start(block, pair):
         dest = lax.rem(block + pair, 4)
         return (dest * 6 + pair * 2) * HEAD, dest
 
-    def partial_block(block, emit):
+    def cot_block(block, emit, send=None):
         image, run = block // 2, lax.rem(block, 2)
         triple = pl.ds(pl.multiple_of(run * 3 * HEAD, 3 * HEAD), 3 * HEAD)
+        for pair in range(3):
+            start, _ = run_start(block, pair)
+            hidden = pl.ds(pl.multiple_of(start, 2 * HEAD), 2 * HEAD)
+            for im in range(2):
+                values = dot_nt(c_ref[im], wdown_ref[hidden, :])
+                for j in range(2):
+                    emit(3 + 2 * pair + j, 2 + im, values[:, j * HEAD : (j + 1) * HEAD])
+            if send is not None:
+                for j in range(2):
+                    send(3 + 2 * pair + j)
+        values = dot_nt(c_ref[image], wout_ref[triple, :])
+        for z in range(3):
+            emit(z, 3, values[:, z * HEAD : (z + 1) * HEAD])
+
+    def x_block(block, emit):
+        image, run = block // 2, lax.rem(block, 2)
         for part in range(3):
             start = part * 6 * HEAD + run * 3 * HEAD
             values = dot(x_ref[image], wq_ref[:, pl.ds(pl.multiple_of(start, HEAD), 3 * HEAD)])
             for z in range(3):
                 emit(z, part, values[:, z * HEAD : (z + 1) * HEAD])
-        values = dot_nt(c_ref[image], wout_ref[triple, :])
-        for z in range(3):
-            emit(z, 3, values[:, z * HEAD : (z + 1) * HEAD])
         for pair in range(3):
             start, _ = run_start(block, pair)
             hidden = pl.ds(pl.multiple_of(start, 2 * HEAD), 2 * HEAD)
@@ -246,9 +223,6 @@
                 values = dot(x_ref[im], wup_ref[:, hidden])
                 for j in range(2):
                     emit(3 + 2 * pair + j, im, values[:, j * HEAD : (j + 1) * HEAD])
-                values = dot_nt(c_ref[im], wdown_ref[hidden, :])
-                for j in range(2):
-                    emit(3 + 2 * pair + j, 2 + im, values[:, j * HEAD : (j + 1) * HEAD])
 
     def at(ref, p, part, parts=1):
         return ref.at[span(p, part, parts)]
@@ -287,21 +261,8 @@
             left,
         )
 
-    def turn_order(i):
-        return lax.rem(i + 2, 3) * 3 + i // 3
-
     def emit_opp(p, part, values):
         opp[span(p, part)] = values.astype(BF16)
-
-    partial_block(xo, emit_opp)
-
-    def send_opp(i, carry):
-        p = turn_order(i)
-        opp_right(p).start()
-        opp_left(p).start()
-        return carry
-
-    lax.fori_loop(0, PIECES, send_opp, 0)
 
     def emit_right(p, part, values):
         if part >= 2:
@@ -309,115 +270,171 @@
         else:
             right_acc[pl.ds(p * half_rows + part * patches, patches)] = values
 
-    partial_block(xr, emit_right)
-
     def emit_left(p, part, values):
         if part < 2:
             left_send[span(p, part)] = values.astype(BF16)
         else:
             left_acc[pl.ds(p * half_rows + (part - 2) * patches, patches)] = values
 
-    partial_block(xl, emit_left)
-
-    def pass_on(i, carry):
-        p = turn_order(i)
-        side_right(p, 1).start()
-        side_left(p, 0).start()
+    def emit_own(p, part, values):
+        own[span(p, part)] = values
+
+    normed_sums = norm_sums
+    for k in range(1, cols):
+        norm_copy(k).wait_recv()
+        normed_sums = normed_sums + norm_in[k - 1]
+    normed_sums = normed_sums * (1.0 / (width * cols))
+    average = normed_sums[0:1]
+    factor = lax.rsqrt(normed_sums[1:2] - average * average + EPS)
+    turned = exact_nt(eye, jnp.where(which == 0, average, factor))
+    avg_ref[...] = jnp.broadcast_to(turned[:, 0:1], avg_ref.shape)
+    factor_ref[...] = jnp.broadcast_to(turned[:, 1:2], factor_ref.shape)
+    normed = (inputs_wide - turned[:, 0:1]) * turned[:, 1:2]
+    x_ref[:, patch_rows(row), :] = (
+        (normed * ln_ref[...]).astype(BF16).reshape(images, own_patches, width)
+    )
+    row_send(1, x_ref)
+
+    row_arrive(0, c_ref)
+    loads[0].wait()
+    loads[1].wait()
+    cot_block(xo, emit_opp, lambda p: opp_left(p).start())
+    cot_block(xr, emit_right, lambda p: side_right(p, 1).start())
+    loads[2].wait()
+    loads[3].wait()
+    row_arrive(1, x_ref)
+    x_block(xo, emit_opp)
+    for p in range(3):
+        opp_left(p).start()
+    for i in range(2):
+        opp_right(SUM_ORDER[i]).start()
+    x_block(xl, emit_left)
+    for i in range(2):
+        side_left(SUM_ORDER[i], 0).start()
+    cot_block(xl, emit_left)
+    x_block(xr, emit_right)
+    cot_block(xi, emit_own)
+    x_block(xi, emit_own)
+
+    def pass_on(i):
+        p = SUM_ORDER[i]
+        if i + 2 < PIECES:
+            opp_right(SUM_ORDER[i + 2]).start()
+            side_left(SUM_ORDER[i + 2], 0).start()
+        if p < 3:
+            side_right(p, 1).start()
+        opp_left(p).wait_recv()
+        left_send[span(p, 2, 2)] = (
+            left_acc[half_span(p)] + half_right[half_span(p)].astype(F32)
+        ).astype(BF16)
+        side_left(p, 1).start()
         opp_right(p).wait_recv()
         right_send[span(p, 0, 2)] = (
             right_acc[half_span(p)] + half_left[half_span(p)].astype(F32)
         ).astype(BF16)
         side_right(p, 0).start()
-        opp_left(p).wait_recv()
-        left_send[span(p, 2, 2)] = (
-            left_acc[half_span(p)] + half_right[half_span(p)].astype(F32)
-        ).astype(BF16)
-        side_left(p, 1).start()
-        return carry
-
-    lax.fori_loop(0, PIECES, pass_on, 0)
-
-    def emit_own(p, part, values):
-        own[span(p, part)] = values
-
-    partial_block(xi, emit_own)
+
+    z_up, z_down = (dp, row, xi * SIDE + lax.rem(zi + 1, SIDE)), (
+        dp, row, xi * SIDE + lax.rem(zi + 3, SIDE)
+    )
+
+    def chain_copy(p, up):
+        slot = p if up else jnp.where(zi - 1 == owner_z(p), PIECES + owner_slot(p), p)
+        return remote(
+            at(z_send, p, 0, 4),
+            at(z_recv, slot, 0, 4),
+            s_z.at[p],
+            r_z.at[slot],
+            z_up if up else z_down,
+        )
+
+    def chain_pass(p, up):
+        here = span(p, 0, 4)
+        chain_copy(p, True).wait_recv()
+        z_send[here] = (own[here] + z_recv[here].astype(F32)).astype(BF16)
+        chain_copy(p, up).start()
+
+    def chain_end(p, up):
+        here = span(p, 0, 4)
+        z_send[here] = own[here].astype(BF16)
+        chain_copy(p, up).start()
+
+    for turn in range(PIECES + BEHIND + 2):
+        if turn < PIECES:
+            pass_on(turn)
+        i = turn - BEHIND
+        if 0 <= i < PIECES:
+            p = SUM_ORDER[i]
+            for half in range(2):
+                side_right(p, half).wait_recv()
+                side_left(p, half).wait_recv()
+            here = span(p, 0, 4)
+            own[here] = own[here] + full_left[here].astype(F32) + full_right[here].astype(F32)
+            if owner_z(p) > 0:
+                pl.when(zi == 0)(functools.partial(chain_end, p, True))
+            if owner_z(p) < 3:
+                pl.when(zi == 3)(functools.partial(chain_end, p, False))
+        for lag in range(1, 3):
+            if 0 <= i - lag < PIECES:
+                p = SUM_ORDER[i - lag]
+                if owner_z(p) > lag:
+                    pl.when(zi == lag)(functools.partial(chain_pass, p, True))
+                if owner_z(p) < 3 - lag:
+                    pl.when(zi == 3 - lag)(functools.partial(chain_pass, p, False))
+
     for im in range(images):
         here = slice(im * patches, (im + 1) * patches)
         x_turned[:, here] = x_ref[im].T
         c_turned[:, here] = c_ref[im].T
 
-    def z_copy(p, k):
-        return remote(
-            at(z_send, p, 0, 4),
-            z_recv.at[k - 1, owner_slot(p)],
-            s_z.at[p],
-            r_z.at[k - 1, owner_slot(p)],
-            z_peer(k),
-        )
-
-    for i in range(PIECES):
-        p = ((i + 2) % 3) * 3 + i // 3
-        for half in range(2):
-            side_right(p, half).wait_recv()
-            side_left(p, half).wait_recv()
-        here = span(p, 0, 4)
-        own[here] = own[here] + full_left[here].astype(F32) + full_right[here].astype(F32)
-        for k in range(1, SIDE):
-
-            @pl.when(lax.rem(zi + k, SIDE) == owner_z(p))
+    def arrived(p, slot):
+        for come, place in ((zi > 0, p), (zi < 3, PIECES + slot)):
+
+            @pl.when(come)
             def _():
-                z_send[here] = own[here].astype(BF16)
-                z_copy(p, k).start()
-
-    def arrived(p, slot):
-        for k in range(1, SIDE):
-            remote(
-                at(z_send, 0, 0, 4),
-                z_recv.at[k - 1, slot],
-                s_z.at[0],
-                r_z.at[k - 1, slot],
-                z_peer(k),
-            ).wait_recv()
-
-    def summed(p, slot, part):
-        total = own[span(p, part)]
-        here = slice(part * patches, (part + 1) * patches)
-        for k in range(1, SIDE):
-            total = total + z_recv[k - 1, slot, here].astype(F32)
-        return total
+                there, here = span(place, 0, 4), span(p, 0, 4)
+                remote(
+                    at(z_send, 0, 0, 4), z_recv.at[there], s_z.at[0], r_z.at[place], z_up
+                ).wait_recv()
+                own[here] = own[here] + z_recv[there].astype(F32)
+
+    def summed(p, part):
+        return own[span(p, part)]
 
     def own_ag(p, way):
         peer = right if way == 0 else left
         return remote(g_ref.at[xi, p], g_ref.at[xi, p], s_own.at[way, p], r_own.at[way, p], peer)
 
-    def z_ag(p, k):
-        return remote(g_ref.at[xi, p], g_ref.at[xi, p], s_zag.at[k - 1, p], r_zag.at[p], z_peer(k))
+    def z_ag(p, up):
+        way = 0 if up else 1
+        peer = z_up if up else z_down
+        return remote(g_ref.at[xi, p], g_ref.at[xi, p], s_zag.at[way, p], r_zag.at[p], peer)
 
     def launch(p):
         for way in range(2):
             own_ag(p, way).start()
-        for k in range(1, SIDE):
-            z_ag(p, k).start()
+        pl.when(zi < 3)(lambda: z_ag(p, True).start())
+        pl.when(zi > 0)(lambda: z_ag(p, False).start())
 
     def hidden_units(p, slot):
         arrived(p, slot)
         for im in range(2):
-            value, slope = gelu_both(summed(p, slot, im))
+            value, slope = gelu_both(summed(p, im))
             g_ref[xi, p, im] = value.astype(BF16)
-            g_ref[xi, p, 2 + im] = (summed(p, slot, 2 + im) * slope).astype(BF16)
+            g_ref[xi, p, 2 + im] = (summed(p, 2 + im) * slope).astype(BF16)
         launch(p)
 
     scale = HEAD ** (-0.5)
 
     def attention(p):
         arrived(p, 0)
-        query_hat, query_factor = normalize(summed(p, 0, 0))
-        key_hat, key_factor = normalize(summed(p, 0, 1))
+        query_hat, query_factor = normalize(summed(p, 0))
+        key_hat, key_factor = normalize(summed(p, 1))
         query_gain, key_gain = gain_ref[0:1, :], gain_ref[1:2, :]
         query = (query_hat * query_gain).astype(BF16)
         key = (key_hat * key_gain).astype(BF16)
-        value = summed(p, 0, 2).astype(BF16)
-        grad = summed(p, 0, 3).astype(BF16)
+        value = summed(p, 2).astype(BF16)
+        grad = summed(p, 3).astype(BF16)
         expo = jnp.exp(dot_nt(query, key) * scale)
         weights = expo / jnp.sum(expo, -1, keepdims=True)
         weights_half = weights.astype(BF16)
@@ -439,8 +456,8 @@
 
     @pl.when(zi < 3)
     def _():
+        attention(zi)
         hidden_units(zi + 3, 1)
-        attention(zi)
 
     @pl.when(zi == 3)
     def _():
@@ -484,15 +501,16 @@
     own_count = jnp.where(zi == 3, 3, 2)
 
     def piece_at(i):
-        piece, start = i * 0, 0
-        for step in range(SIDE):
-            z = lax.rem(zi + step, SIDE)
-            count = jnp.where(z == 3, 3, 2)
-            slot = i - start
-            named = jnp.where(z == 3, 6 + slot, z + 3 * slot)
-            piece = jnp.where((slot >= 0) & (slot < count), named, piece)
-            start = start + count
+        piece = i * 0
+        for place in range(PIECES):
+            named = GATHER_ORDER[0][place]
+            for z in range(1, SIDE):
+                named = jnp.where(zi == z, GATHER_ORDER[z][place], named)
+            piece = jnp.where(i == place, named, piece)
         return piece
+
+    def owner_of(p):
+        return jnp.where(p < 3, p, jnp.where(p < 6, p - 3, 3))
 
     dp_right = (lax.rem(dp + 1, dps), row, col)
     dp_left = (lax.rem(dp + dps - 1, dps), row, col)
@@ -646,9 +664,12 @@
         @pl.when((ahead >= own_count) & (ahead < PIECES))
         def _():
             p = piece_at(ahead)
-            z_ag(p, 1).wait_recv()
+            z_ag(p, True).wait_recv()
             for way in range(2):
                 own_ag(p, way).start()
+            owner = owner_of(p)
+            pl.when((owner < zi) & (zi < 3))(lambda: z_ag(p, True).start())
+            pl.when((owner > zi) & (zi > 0))(lambda: z_ag(p, False).start())
 
         @pl.when(i < PIECES)
         def _():
@@ -687,7 +708,7 @@
 
         def each_pass(k, carry):
             block = lax.rem(xi + k, 4)
-            turn = i - jnp.where(k == 2, 3, 1)
+            turn = i - LATE - jnp.where(k == 2, 2, 0)
             p = piece_at(turn)
             live = (turn >= 0) & (turn < PIECES)
 
@@ -706,33 +727,37 @@
 
     lax.fori_loop(0, STEPS, step, 0)
 
-    for which, acc in enumerate((out_acc, norm_acc)):
-        for im in range(images):
-            here = slice(im * patches, (im + 1) * patches)
-            row_out[which, im] = acc[here].astype(BF16)
-
-    def row_copy(k):
-        there = lax.rem(row + k, rows)
-        return remote(
-            row_out.at[:, :, pl.ds(pl.multiple_of(there * own_patches, own_patches), own_patches), :],
-            row_in.at[k - 1],
-            s_row.at[k - 1],
-            r_row.at[k - 1],
-            row_peer(k),
-        )
-
-    for k in range(1, rows):
-        row_copy(k).start()
-    for k in range(1, rows):
-        row_copy(k).wait_recv()
-
-    def row_total(which, acc):
+    accs = (out_acc, norm_acc)
+    parity = lax.rem(row, 2)
+
+    def row_part(acc, r, im):
+        start = im * patches + r * own_patches
+        return acc[pl.ds(pl.multiple_of(start, own_patches), own_patches)]
+
+    core_copy = remote(core_out, core_in, s_core.at[0], r_core.at[0], mate)
+    row_copy = remote(row_out, row_in, s_row.at[0], r_row.at[0], cross)
+    other_high = lax.rem(row // 2 + 1, 2)
+    if rows > 1:
+        for w, acc in enumerate(accs):
+            for im in range(images):
+                for j, high_z in enumerate((other_high, row // 2)):
+                    core_out[j, w, im] = row_part(acc, high_z * 2 + 1 - parity, im).astype(BF16)
+        core_copy.start()
+        core_copy.wait_recv()
+        for w, acc in enumerate(accs):
+            for im in range(images):
+                row_out[w, im] = (
+                    row_part(acc, lax.rem(row + 2, rows), im) + core_in[0, w, im].astype(F32)
+                ).astype(BF16)
+        row_copy.start()
+        row_copy.wait_recv()
+
+    def row_total(w, acc):
         parts = []
         for im in range(images):
-            start = im * patches + row * own_patches
-            total = acc[pl.ds(pl.multiple_of(start, own_patches), own_patches)]
-            for k in range(1, rows):
-                total = total + row_in[k - 1, which, im].astype(F32)
+            total = row_part(acc, row, im)
+            if rows > 1:
+                total = total + core_in[1, w, im].astype(F32) + row_in[w, im].astype(F32)
             parts.append(total)
         return jnp.concatenate(parts, 0)
 
@@ -741,8 +766,6 @@
     normed = (inputs_wide - average) * factor
     norm_grad = row_total(1, norm_acc)
     scaled = norm_grad * ln_ref[...]
-    ones = jnp.ones((8, width), F32)
-    which = lax.broadcasted_iota(jnp.int32, (8, tokens), 0)
     stats = jnp.where(which == 0, exact_nt(ones, scaled), exact_nt(ones, scaled * normed))
     stat_mine[...] = stats
 
@@ -776,10 +799,6 @@
         stat_copy(k).wait_recv()
         stats = stats + stat_in[k - 1]
     stats = stats * (1.0 / (width * cols))
-    eye = (
-        lax.broadcasted_iota(jnp.int32, (tokens, tokens), 0)
-        == lax.broadcasted_iota(jnp.int32, (tokens, tokens), 1)
-    ).astype(F32)
     turned = exact_nt(eye, stats)
     centre, along = turned[:, 0:1], turned[:, 1:2]
     input_grad = cot_ref[...].astype(F32).reshape(tokens, width) + factor * (
@@ -841,31 +860,31 @@
     if dps > 1:
         lax.fori_loop(0, UNITS, finish_unit, 0)
     for p in range(PIECES):
-
-        @pl.when(zi != owner_z(p))
-        def _():
-            z_copy(p, 1).wait_send()
-
-        @pl.when(zi == owner_z(p))
-        def _():
-            for k in range(1, SIDE):
-                z_ag(p, k).wait_send()
+        pl.when(zi != owner_z(p))(lambda: chain_copy(p, True).wait_send())
+        if owner_z(p) < 3:
+            pl.when((zi >= owner_z(p)) & (zi < 3))(lambda: z_ag(p, True).wait_send())
+        if owner_z(p) > 0:
+            pl.when((zi <= owner_z(p)) & (zi > 0))(lambda: z_ag(p, False).wait_send())
 
     for k in range(1, cols):
         gain_copy(k).wait_send()
         stat_copy(k).wait_send()
-    for k in range(1, rows):
-        row_copy(k).wait_send()
+    for k in range(1, cols):
+        norm_copy(k).wait_send()
+    if rows > 1:
+        core_copy.wait_send()
+        row_copy.wait_send()
+        for w, ref in enumerate((c_ref, x_ref)):
+            for turn in range(3):
+                row_gather(w, ref, turn).wait_send()
     for k in range(1, teams):
         last_copy(k).wait_send()
 
 
-def exchange(
-    x_all, c_all, w_qkv, w_up, w_out, w_down, qk_gain, features, cotangent, ln_gain, average, factor
-):
+def exchange(w_qkv, w_up, w_out, w_down, qk_gain, features, cotangent, ln_gain):
     dps, rows, cols = lax.axis_size("dp"), lax.axis_size("row"), lax.axis_size("col")
-    images, patches, width = x_all.shape
-    own_patches = features.shape[1]
+    images, own_patches, width = features.shape
+    patches = own_patches * rows
     tokens = images * own_patches
     teams = dps * rows
     dma = pltpu.SemaphoreType.DMA
@@ -873,7 +892,7 @@
     half = max(PIECES * 2 * patches, UNITS * width // 2)
     units = UNITS * width
     struct = jax.ShapeDtypeStruct
-    others, mates, peers = max(teams - 1, 1), max(rows - 1, 1), cols - 1
+    others, peers = max(teams - 1, 1), cols - 1
     return pl.pallas_call(
         functools.partial(core_kernel, dps, rows, cols),
         out_shape=(
@@ -886,9 +905,17 @@
             struct((3 * HEAD // 2, width), F32),
             struct((6 * HEAD, width), F32),
         ),
-        in_specs=vmem(12),
+        in_specs=[pl.BlockSpec(memory_space=pl.ANY)] * 4 + vmem(4),
         out_specs=tuple(vmem(8)),
         scratch_shapes=[
+            pltpu.VMEM((images, patches, width), BF16),
+            pltpu.VMEM((images, patches, width), BF16),
+            pltpu.VMEM(w_qkv.shape, BF16),
+            pltpu.VMEM(w_up.shape, BF16),
+            pltpu.VMEM(w_out.shape, BF16),
+            pltpu.VMEM(w_down.shape, BF16),
+            pltpu.VMEM((tokens, HEAD), F32),
+            pltpu.VMEM((tokens, HEAD), F32),
             pltpu.VMEM((SIDE, PIECES, 4, patches, HEAD), BF16),
             pltpu.VMEM((whole, HEAD), BF16),
             pltpu.VMEM((whole, HEAD), BF16),
@@ -901,7 +928,7 @@
             pltpu.VMEM((PIECES * 4 * patches, HEAD), BF16),
             pltpu.VMEM((PIECES * 4 * patches, HEAD), BF16),
             pltpu.VMEM((PIECES * 4 * patches, HEAD), BF16),
-            pltpu.VMEM((SIDE - 1, 3, 4 * patches, HEAD), BF16),
+            pltpu.VMEM(((PIECES + 3) * 4 * patches, HEAD), BF16),
             pltpu.VMEM((units // 2, HEAD), BF16),
             pltpu.VMEM((units // 2, HEAD), BF16),
             pltpu.VMEM((units, HEAD), BF16),
@@ -910,8 +937,12 @@
             pltpu.VMEM((width, images * patches), BF16),
             pltpu.VMEM((images * patches, width), F32),
             pltpu.VMEM((images * patches, width), F32),
-            pltpu.VMEM((2, images, patches, width), BF16),
-            pltpu.VMEM((mates, 2, images, own_patches, width), BF16),
+            pltpu.VMEM((2, 2, images, own_patches, width), BF16),
+            pltpu.VMEM((2, 2, images, own_patches, width), BF16),
+            pltpu.VMEM((2, images, own_patches, width), BF16),
+            pltpu.VMEM((2, images, own_patches, width), BF16),
+            pltpu.VMEM((8, tokens), F32),
+            pltpu.VMEM((peers, 8, tokens), F32),
             pltpu.VMEM((8, HEAD), F32),
             pltpu.VMEM((peers, 8, HEAD), F32),
             pltpu.VMEM((8, tokens), F32),
@@ -923,19 +954,26 @@
             dma((2, 2, PIECES)),
             dma((2, 2, PIECES)),
             dma((PIECES,)),
-            dma((SIDE - 1, 3)),
+            dma((PIECES + 3,)),
             dma((2, PIECES)),
             dma((2, PIECES)),
             dma((2, PIECES)),
             dma((2, PIECES)),
-            dma((SIDE - 1, PIECES)),
+            dma((2, PIECES)),
             dma((PIECES,)),
+            dma((4,)),
+            dma((peers,)),
+            dma((peers,)),
+            dma((2, 3)),
+            dma((2, 3)),
+            dma((1,)),
+            dma((1,)),
             dma((2, UNITS)),
             dma((2, UNITS)),
             dma((2, 2, UNITS)),
             dma((2, 2, UNITS)),
-            dma((mates,)),
-            dma((mates,)),
+            dma((1,)),
+            dma((1,)),
             dma((peers,)),
             dma((peers,)),
             dma((peers,)),
@@ -944,23 +982,18 @@
             dma((others,)),
         ],
         compiler_params=pltpu.CompilerParams(
-            collective_id=1, has_side_effects=True, vmem_limit_bytes=VMEM_BYTES
+            collective_id=0, has_side_effects=True, vmem_limit_bytes=VMEM_BYTES
         ),
         name="exchange",
-    )(
-        x_all, c_all, w_qkv, w_up, w_out, w_down, qk_gain,
-        features, cotangent, ln_gain, average, factor,
-    )
+    )(w_qkv, w_up, w_out, w_down, qk_gain, features, cotangent, ln_gain)
 
 
 def on_device(features, ln_gain, w_qkv, qk_gain, w_up, w_out, w_down, cotangent):
     images, patches, width = features.shape
     head_cols = w_qkv.shape[2]
-    x_all, c_all, average, factor = gather_inputs(features, ln_gain, cotangent)
     qkv_flat = w_qkv.reshape(width, 3 * head_cols)
     output, input_grad, ln_grad, gains, qkv_units, up_grad, out_grad, down_grad = exchange(
-        x_all, c_all, qkv_flat, w_up, w_out, w_down, qk_gain,
-        features, cotangent, ln_gain.reshape(1, width), average, factor,
+        qkv_flat, w_up, w_out, w_down, qk_gain, features, cotangent, ln_gain.reshape(1, width)
     )
     units = qkv_units.reshape(3, 2, width, HEAD)
     whole, split = units[:, 0], units[:, 1]

time: 317 us -> 259 us (0.82)
  Pallas kernels: 301 us -> 242 us
    pallas_call x1 -> x0, Pallas kernels: 30.3 us -> none  [gather_inputs(): pl.pallas_call(functools.partial(pre_kernel, rows, cols), out_shape=(whol...]
    pallas_call x1, Pallas kernels: 271 us -> 242 us  [exchange(): pl.pallas_call(functools.partial(core_kernel, dps, rows, cols), out_shape...]
where the time goes in v3:
time: 259 us; the launch traced here: 258 us
  Pallas kernels  242 us (93%)
  local copies, waits for them, and re-layouts  12.9 us (5%)
    pallas_call x1, Pallas kernels, exchange(): pl.pallas_call(functools.partial(core_kernel, dps, rows, cols), out_shape...  242 us
    unnamed x20, local copies, waits for them, and re-layouts  7.37 us

profile of v3, /device:TPU:1, one launch (start us, length us, event | category | flops | bytes accessed | tf_op | source)
XLA Modules:
  0.0 257.7 jit_solution(2817872985080286177)
XLA Ops:
  0.6 2.8 %copy.19 = bf16[384,3,768]{0,2,1:T(8,128)(2,1)S(1)} copy(bf16[384,3,768]{2,0,1:T(8,128)(2,1)} %param.10) | data formatting | bytes 3538944 | tf_op args[2]
  3.4 0.0 copy-start.5
  3.4 2.4 copy.20.wq_hbm
  5.8 0.0 copy-done.5
  5.8 0.6 reshape.29.ln_ref
  6.4 241.8 %exchange.1 = (bf16[2,64,384]{2,1,0:T(8,128)(2,1)}, bf16[2,64,384]{2,1,0:T(8,128)(2,1)}, f32[1,384]{1,0:T(1,128)}, f32[8,128]{1,0:T(8,128)}, f32[6,384,128]{2,1,...) custom-call(bf16[384,2304]{1,0:T(8,128)(2,1)} %copy.20.wq_hbm, bf16[384,3072]{1,0:T(8,128)(2,1)} %wup_hbm.1, ...), custom_call_target="tpu_custom_call" | custom-call | tf_op jit(solution)/shard_map/exchange/pallas_call | solution.py:896
  248.2 1.2 reduce
  249.4 1.2 slice.15
  250.7 1.3 fusion.1
  252.0 0.2 copy.24
  252.3 0.2 copy.23
  252.5 0.0 copy-start.4
  252.5 0.0 copy-start.3
  252.5 0.0 copy-start.1
  252.5 1.0 fusion
  253.5 0.0 copy-done.4
  253.5 0.6 copy.30
  254.1 0.0 copy-done.3
  254.2 0.6 copy.31
  254.8 0.0 copy-done.1
  254.8 1.0 copy.32
  255.8 0.1 copy-done.2
  255.9 0.7 copy.33
  256.6 1.0 copy.34
  (4 shorter events, 0.0 us)
Async XLA Ops:
  3.4 2.4 copy-start.5
  252.5 1.0 copy-start.4
  252.5 1.7 copy-start.3
  252.5 2.3 copy-start.1
  254.8 1.1 copy-start.2
  254.8 1.8 copy-start

commit v4 on v3

--- a/solution.py
+++ b/solution.py
@@ -57,11 +57,20 @@
     )
 
 
-def greet(peers):
+def lane_sums(values):
+    ones = jnp.ones((8, values.shape[1]), BF16)
+    high = values.astype(BF16)
+    low = (values - high.astype(F32)).astype(BF16)
+    return dot_nt(ones, high) + dot_nt(ones, low)
+
+
+def greet(peers, meanwhile):
     barrier = pltpu.get_barrier_semaphore()
     for peer in peers:
         pl.semaphore_signal(barrier, inc=1, device_id=peer, device_id_type=MESH)
+    result = meanwhile()
     pl.semaphore_wait(barrier, len(peers))
+    return result
 
 
 def remote(src, dst, send, recv, peer):
@@ -89,14 +98,13 @@
 
 UNITS = 20
 BEHIND = 2
-LATE = 1
-STEPS = PIECES + 2 + LATE
-SUM_ORDER = (6, 0, 7, 3, 8, 1, 2, 4, 5)
+STEPS = PIECES + 2
+SUM_ORDER = (6, 0, 7, 3, 1, 2, 8, 4, 5)
 GATHER_ORDER = (
     (0, 3, 1, 4, 2, 5, 6, 7, 8),
     (1, 4, 0, 2, 3, 5, 6, 7, 8),
-    (2, 5, 1, 6, 4, 7, 0, 8, 3),
-    (6, 7, 8, 2, 5, 1, 4, 0, 3),
+    (2, 5, 1, 6, 0, 7, 4, 8, 3),
+    (6, 7, 8, 2, 5, 1, 0, 4, 3),
 )
 
 
@@ -110,10 +118,10 @@
     dhalf_left, dhalf_right, dfull_left, dfull_right,
     x_turned, c_turned, out_acc, norm_acc, core_out, core_in, row_out, row_in,
     norm_mine, norm_in,
-    gain_mine, gain_in, stat_mine, stat_in, last_mine, last_in,
+    gain_mine, gain_in, stat_mine, stat_in, last_mine, last_in, both_mine, both_in,
     s_opp, r_half, s_side, r_full, s_z, r_z, s_own, r_own, s_fwd, r_fwd, s_zag, r_zag,
     s_load, s_norm, r_norm, s_rowg, r_rowg, s_core, r_core,
-    s_dopp, r_dhalf, s_dside, r_dfull, s_row, r_row, s_gain, r_gain, s_stat, r_stat, s_last, r_last,
+    s_dopp, r_dhalf, s_dside, r_dfull, s_row, r_row, s_gain, r_gain, s_stat, r_stat, s_last, r_last, s_both, r_both,
 ):
     dp, row, col = lax.axis_index("dp"), lax.axis_index("row"), lax.axis_index("col")
     xi, zi = col // SIDE, lax.rem(col, SIDE)
@@ -143,8 +151,6 @@
     ]
     for load in loads:
         load.start()
-    greet([col_peer(k) for k in range(1, cols)] + [team_peer(k) for k in range(1, teams)])
-
     def patch_rows(r):
         return pl.ds(pl.multiple_of(r * own_patches, own_patches), own_patches)
 
@@ -166,15 +172,21 @@
             row_gather(which, ref, 0).wait_recv()
             row_gather(which, ref, 2).wait_recv()
 
-    c_ref[:, patch_rows(row), :] = cot_ref[...]
+    inputs_wide = feat_ref[...].astype(F32).reshape(tokens, width)
+    which = lax.broadcasted_iota(jnp.int32, (8, tokens), 0)
+
+    def own_sums():
+        c_ref[:, patch_rows(row), :] = cot_ref[...]
+        sums = jnp.where(
+            which == 0, lane_sums(inputs_wide), lane_sums(inputs_wide * inputs_wide)
+        )
+        norm_mine[...] = sums
+        return sums
+
+    norm_sums = greet(
+        [col_peer(k) for k in range(1, cols)] + [team_peer(k) for k in range(1, teams)], own_sums
+    )
     row_send(0, c_ref)
-    inputs_wide = feat_ref[...].astype(F32).reshape(tokens, width)
-    ones = jnp.ones((8, width), F32)
-    which = lax.broadcasted_iota(jnp.int32, (8, tokens), 0)
-    norm_sums = jnp.where(
-        which == 0, exact_nt(ones, inputs_wide), exact_nt(ones, inputs_wide * inputs_wide)
-    )
-    norm_mine[...] = norm_sums
 
     def norm_copy(k):
         return remote(
@@ -211,9 +223,9 @@
 
     def x_block(block, emit):
         image, run = block // 2, lax.rem(block, 2)
+        triple = pl.ds(pl.multiple_of(run * 3 * HEAD, 3 * HEAD), 3 * HEAD)
         for part in range(3):
-            start = part * 6 * HEAD + run * 3 * HEAD
-            values = dot(x_ref[image], wq_ref[:, pl.ds(pl.multiple_of(start, HEAD), 3 * HEAD)])
+            values = dot(x_ref[image], wq_ref[part, :, triple])
             for z in range(3):
                 emit(z, part, values[:, z * HEAD : (z + 1) * HEAD])
         for pair in range(3):
@@ -279,6 +291,11 @@
     def emit_own(p, part, values):
         own[span(p, part)] = values
 
+    row_arrive(0, c_ref)
+    loads[0].wait()
+    loads[1].wait()
+    cot_block(xo, emit_opp, lambda p: opp_left(p).start())
+    cot_block(xr, emit_right, lambda p: side_right(p, 1).start())
     normed_sums = norm_sums
     for k in range(1, cols):
         norm_copy(k).wait_recv()
@@ -295,11 +312,8 @@
     )
     row_send(1, x_ref)
 
-    row_arrive(0, c_ref)
-    loads[0].wait()
-    loads[1].wait()
-    cot_block(xo, emit_opp, lambda p: opp_left(p).start())
-    cot_block(xr, emit_right, lambda p: side_right(p, 1).start())
+    cot_block(xl, emit_left)
+    cot_block(xi, emit_own)
     loads[2].wait()
     loads[3].wait()
     row_arrive(1, x_ref)
@@ -311,10 +325,13 @@
     x_block(xl, emit_left)
     for i in range(2):
         side_left(SUM_ORDER[i], 0).start()
-    cot_block(xl, emit_left)
     x_block(xr, emit_right)
-    cot_block(xi, emit_own)
     x_block(xi, emit_own)
+
+    for im in range(images):
+        here = slice(im * patches, (im + 1) * patches)
+        x_turned[:, here] = x_ref[im].T
+        c_turned[:, here] = c_ref[im].T
 
     def pass_on(i):
         p = SUM_ORDER[i]
@@ -358,34 +375,6 @@
         here = span(p, 0, 4)
         z_send[here] = own[here].astype(BF16)
         chain_copy(p, up).start()
-
-    for turn in range(PIECES + BEHIND + 2):
-        if turn < PIECES:
-            pass_on(turn)
-        i = turn - BEHIND
-        if 0 <= i < PIECES:
-            p = SUM_ORDER[i]
-            for half in range(2):
-                side_right(p, half).wait_recv()
-                side_left(p, half).wait_recv()
-            here = span(p, 0, 4)
-            own[here] = own[here] + full_left[here].astype(F32) + full_right[here].astype(F32)
-            if owner_z(p) > 0:
-                pl.when(zi == 0)(functools.partial(chain_end, p, True))
-            if owner_z(p) < 3:
-                pl.when(zi == 3)(functools.partial(chain_end, p, False))
-        for lag in range(1, 3):
-            if 0 <= i - lag < PIECES:
-                p = SUM_ORDER[i - lag]
-                if owner_z(p) > lag:
-                    pl.when(zi == lag)(functools.partial(chain_pass, p, True))
-                if owner_z(p) < 3 - lag:
-                    pl.when(zi == 3 - lag)(functools.partial(chain_pass, p, False))
-
-    for im in range(images):
-        here = slice(im * patches, (im + 1) * patches)
-        x_turned[:, here] = x_ref[im].T
-        c_turned[:, here] = c_ref[im].T
 
     def arrived(p, slot):
         for come, place in ((zi > 0, p), (zi < 3, PIECES + slot)):
@@ -454,15 +443,35 @@
 
     gain_mine[...] = jnp.zeros_like(gain_mine)
 
-    @pl.when(zi < 3)
-    def _():
-        attention(zi)
-        hidden_units(zi + 3, 1)
-
-    @pl.when(zi == 3)
-    def _():
-        for j in range(3):
-            hidden_units(6 + j, j)
+    for turn in range(PIECES + BEHIND + 2):
+        if turn < PIECES:
+            pass_on(turn)
+        i = turn - BEHIND
+        if 0 <= i < PIECES:
+            p = SUM_ORDER[i]
+            for half in range(2):
+                side_right(p, half).wait_recv()
+                side_left(p, half).wait_recv()
+            here = span(p, 0, 4)
+            own[here] = own[here] + full_left[here].astype(F32) + full_right[here].astype(F32)
+            if owner_z(p) > 0:
+                pl.when(zi == 0)(functools.partial(chain_end, p, True))
+            if owner_z(p) < 3:
+                pl.when(zi == 3)(functools.partial(chain_end, p, False))
+        for lag in range(1, 3):
+            if 0 <= i - lag < PIECES:
+                p = SUM_ORDER[i - lag]
+                if owner_z(p) > lag:
+                    pl.when(zi == lag)(functools.partial(chain_pass, p, True))
+                if owner_z(p) < 3 - lag:
+                    pl.when(zi == 3 - lag)(functools.partial(chain_pass, p, False))
+        if turn == PIECES:
+            pl.when(zi < 3)(lambda: attention(zi))
+        if turn in (PIECES, PIECES + 1):
+            pl.when(zi == 3)(functools.partial(hidden_units, turn - 3, turn - PIECES))
+
+    pl.when(zi < 3)(lambda: hidden_units(zi + 3, 1))
+    pl.when(zi == 3)(lambda: hidden_units(8, 2))
 
     def gain_copy(k):
         return remote(
@@ -622,10 +631,10 @@
         out_acc[here] += dot(
             g_ref[block, z, 0], wout_ref[pl.ds(pl.multiple_of(head * HEAD, HEAD), HEAD), :]
         )
+        columns = pl.ds(pl.multiple_of(head * HEAD, HEAD), HEAD)
         total = norm_acc[here]
         for part in range(3):
-            columns = pl.ds(pl.multiple_of((part * 6 + head) * HEAD, HEAD), HEAD)
-            total = total + dot_nt(g_ref[block, z, 1 + part], wq_ref[:, columns])
+            total = total + dot_nt(g_ref[block, z, 1 + part], wq_ref[part, :, columns])
         norm_acc[here] = total
 
     def attention_weights(run, z):
@@ -658,6 +667,25 @@
             def _():
                 pass_unit(second, u)
 
+    def passes(i):
+        def each_pass(k, carry):
+            block = lax.rem(xi + k, 4)
+            turn = i - 1 - jnp.where(k == 2, 2, 0)
+            p = piece_at(turn)
+            live = (turn >= 0) & (turn < PIECES)
+
+            @pl.when(live & (p >= 3))
+            def _():
+                pass_hidden(block, p)
+
+            @pl.when(live & (p < 3) & (k >= 2))
+            def _():
+                pass_attention(lax.rem(block, 2), p)
+
+            return carry
+
+        lax.fori_loop(0, SIDE, each_pass, 0)
+
     def step(i, carry):
         ahead = i + 2
 
@@ -706,23 +734,7 @@
 
         lax.fori_loop(0, SIDE, each_block, 0)
 
-        def each_pass(k, carry):
-            block = lax.rem(xi + k, 4)
-            turn = i - LATE - jnp.where(k == 2, 2, 0)
-            p = piece_at(turn)
-            live = (turn >= 0) & (turn < PIECES)
-
-            @pl.when(live & (p >= 3))
-            def _():
-                pass_hidden(block, p)
-
-            @pl.when(live & (p < 3) & (k >= 2))
-            def _():
-                pass_attention(lax.rem(block, 2), p)
-
-            return carry
-
-        lax.fori_loop(0, SIDE, each_pass, 0)
+        passes(i)
         return carry
 
     lax.fori_loop(0, STEPS, step, 0)
@@ -735,7 +747,9 @@
         return acc[pl.ds(pl.multiple_of(start, own_patches), own_patches)]
 
     core_copy = remote(core_out, core_in, s_core.at[0], r_core.at[0], mate)
-    row_copy = remote(row_out, row_in, s_row.at[0], r_row.at[0], cross)
+    row_copies = [
+        remote(row_out.at[w], row_in.at[w], s_row.at[w], r_row.at[w], cross) for w in range(2)
+    ]
     other_high = lax.rem(row // 2 + 1, 2)
     if rows > 1:
         for w, acc in enumerate(accs):
@@ -743,14 +757,63 @@
                 for j, high_z in enumerate((other_high, row // 2)):
                     core_out[j, w, im] = row_part(acc, high_z * 2 + 1 - parity, im).astype(BF16)
         core_copy.start()
+
+    gain = ln_ref[...]
+    stats = jnp.zeros((8, tokens), F32)
+    ln_sum = jnp.zeros((1, width), F32)
+    for r in range(rows):
+        grads = jnp.concatenate([row_part(norm_acc, r, im) for im in range(images)], 0)
+        inputs = x_ref[:, pl.ds(r * own_patches, own_patches), :].astype(F32).reshape(tokens, width)
+        along = grads * inputs
+        stats = jnp.where(which == 2 * r, lane_sums(grads * gain), stats)
+        stats = jnp.where(which == 2 * r + 1, lane_sums(along), stats)
+        ln_sum = ln_sum + jnp.sum(along, 0, keepdims=True)
+    ln_sum = ln_sum / gain
+    stat_mine[...] = stats
+
+    def stat_copy(k):
+        return remote(
+            stat_mine, stat_in.at[k - 1], s_stat.at[k - 1], r_stat.at[k - 1], col_peer(k)
+        )
+
+    for k in range(1, cols):
+        stat_copy(k).start()
+    gains = gain_mine[...]
+    for k in range(1, cols):
+        gain_copy(k).wait_recv()
+        gains = gains + gain_in[k - 1]
+    last_mine[...] = gains
+    runs = width // HEAD
+    for j in range(runs):
+        last_mine[2 + j : 3 + j, :] = ln_sum[:, j * HEAD : (j + 1) * HEAD]
+
+    def last_copy(k):
+        return remote(
+            last_mine, last_in.at[k - 1], s_last.at[k - 1], r_last.at[k - 1], team_peer(k)
+        )
+
+    for k in range(1, teams):
+        last_copy(k).start()
+    if rows > 1:
         core_copy.wait_recv()
-        for w, acc in enumerate(accs):
+        for w in (1, 0):
             for im in range(images):
                 row_out[w, im] = (
-                    row_part(acc, lax.rem(row + 2, rows), im) + core_in[0, w, im].astype(F32)
+                    row_part(accs[w], lax.rem(row + 2, rows), im) + core_in[0, w, im].astype(F32)
                 ).astype(BF16)
-        row_copy.start()
-        row_copy.wait_recv()
+            row_copies[w].start()
+    passes(STEPS)
+    for k in range(1, cols):
+        stat_copy(k).wait_recv()
+        stats = stats + stat_in[k - 1]
+    both_mine[...] = stats
+
+    def both_copy(k):
+        there = (dp, lax.rem(row + k, rows), col)
+        return remote(both_mine, both_in.at[k - 1], s_both.at[k - 1], r_both.at[k - 1], there)
+
+    for k in range(1, rows):
+        both_copy(k).start()
 
     def row_total(w, acc):
         parts = []
@@ -760,51 +823,6 @@
                 total = total + core_in[1, w, im].astype(F32) + row_in[w, im].astype(F32)
             parts.append(total)
         return jnp.concatenate(parts, 0)
-
-    inputs_wide = feat_ref[...].astype(F32).reshape(tokens, width)
-    average, factor = avg_ref[:, 0:1], factor_ref[:, 0:1]
-    normed = (inputs_wide - average) * factor
-    norm_grad = row_total(1, norm_acc)
-    scaled = norm_grad * ln_ref[...]
-    stats = jnp.where(which == 0, exact_nt(ones, scaled), exact_nt(ones, scaled * normed))
-    stat_mine[...] = stats
-
-    def stat_copy(k):
-        return remote(
-            stat_mine, stat_in.at[k - 1], s_stat.at[k - 1], r_stat.at[k - 1], col_peer(k)
-        )
-
-    for k in range(1, cols):
-        stat_copy(k).start()
-    gains = gain_mine[...]
-    for k in range(1, cols):
-        gain_copy(k).wait_recv()
-        gains = gains + gain_in[k - 1]
-    last_mine[:, 0:HEAD] = gains
-    last_mine[:, HEAD:] = jnp.broadcast_to(
-        jnp.sum(norm_grad * normed, 0, keepdims=True), (8, width)
-    )
-
-    def last_copy(k):
-        return remote(
-            last_mine, last_in.at[k - 1], s_last.at[k - 1], r_last.at[k - 1], team_peer(k)
-        )
-
-    for k in range(1, teams):
-        last_copy(k).start()
-    output_ref[...] = (
-        (inputs_wide + row_total(0, out_acc)).astype(BF16).reshape(images, own_patches, width)
-    )
-    for k in range(1, cols):
-        stat_copy(k).wait_recv()
-        stats = stats + stat_in[k - 1]
-    stats = stats * (1.0 / (width * cols))
-    turned = exact_nt(eye, stats)
-    centre, along = turned[:, 0:1], turned[:, 1:2]
-    input_grad = cot_ref[...].astype(F32).reshape(tokens, width) + factor * (
-        scaled - centre - normed * along
-    )
-    input_grad_ref[...] = input_grad.astype(BF16).reshape(images, own_patches, width)
 
     def unit_total(u):
         here = unit_span(u)
@@ -834,12 +852,35 @@
         out_ref[0:mid, :] = split[mid:]
         out_ref[mid : HEAD + mid, :] = whole
 
+    average, factor = avg_ref[:, 0:1], factor_ref[:, 0:1]
+    normed = (inputs_wide - average) * factor
+    for k in range(1, rows):
+        both_copy(k).wait_recv()
+        stats = stats + both_in[k - 1]
+    stats = stats * (1.0 / (width * cols))
+    centre_row = jnp.sum(jnp.where(which == 2 * row, stats, 0.0), 0, keepdims=True)
+    along_row = jnp.sum(jnp.where(which == 2 * row + 1, stats, 0.0), 0, keepdims=True)
+    turned = exact_nt(eye, jnp.where(which == 0, centre_row, along_row))
+    centre, along = turned[:, 0:1], turned[:, 1:2]
+    if rows > 1:
+        row_copies[1].wait_recv()
+    input_grad = cot_ref[...].astype(F32).reshape(tokens, width) + factor * (
+        row_total(1, norm_acc) * gain - centre - normed * along
+    )
+    input_grad_ref[...] = input_grad.astype(BF16).reshape(images, own_patches, width)
+    if rows > 1:
+        row_copies[0].wait_recv()
+    output_ref[...] = (
+        (inputs_wide + row_total(0, out_acc)).astype(BF16).reshape(images, own_patches, width)
+    )
+
     last = last_mine[...]
     for k in range(1, teams):
         last_copy(k).wait_recv()
         last = last + last_in[k - 1]
-    gains_ref[...] = last[:, 0:HEAD]
-    ln_grad_ref[...] = last[0:1, HEAD:]
+    gains_ref[...] = last[0:2]
+    for j in range(runs):
+        ln_grad_ref[j * HEAD : (j + 1) * HEAD] = last[2 + j]
 
     def finish(p, carry):
         for way in range(2):
@@ -873,7 +914,10 @@
         norm_copy(k).wait_send()
     if rows > 1:
         core_copy.wait_send()
-        row_copy.wait_send()
+        for w in range(2):
+            row_copies[w].wait_send()
+        for k in range(1, rows):
+            both_copy(k).wait_send()
         for w, ref in enumerate((c_ref, x_ref)):
             for turn in range(3):
                 row_gather(w, ref, turn).wait_send()
@@ -892,14 +936,14 @@
     half = max(PIECES * 2 * patches, UNITS * width // 2)
     units = UNITS * width
     struct = jax.ShapeDtypeStruct
-    others, peers = max(teams - 1, 1), cols - 1
+    others, mates, peers = max(teams - 1, 1), max(rows - 1, 1), cols - 1
     return pl.pallas_call(
         functools.partial(core_kernel, dps, rows, cols),
         out_shape=(
             struct(features.shape, BF16),
             struct(features.shape, BF16),
-            struct((1, width), F32),
-            struct((8, HEAD), F32),
+            struct((width,), F32),
+            struct((2, HEAD), F32),
             struct((6, width, HEAD), F32),
             struct((width, 6 * HEAD), F32),
             struct((3 * HEAD // 2, width), F32),
@@ -947,8 +991,10 @@
             pltpu.VMEM((peers, 8, HEAD), F32),
             pltpu.VMEM((8, tokens), F32),
             pltpu.VMEM((peers, 8, tokens), F32),
-            pltpu.VMEM((8, HEAD + width), F32),
-            pltpu.VMEM((others, 8, HEAD + width), F32),
+            pltpu.VMEM((8, HEAD), F32),
+            pltpu.VMEM((others, 8, HEAD), F32),
+            pltpu.VMEM((8, tokens), F32),
+            pltpu.VMEM((mates, 8, tokens), F32),
             dma((2, PIECES)),
             dma((2, PIECES)),
             dma((2, 2, PIECES)),
@@ -972,14 +1018,16 @@
             dma((2, UNITS)),
             dma((2, 2, UNITS)),
             dma((2, 2, UNITS)),
-            dma((1,)),
-            dma((1,)),
+            dma((2,)),
+            dma((2,)),
             dma((peers,)),
             dma((peers,)),
             dma((peers,)),
             dma((peers,)),
             dma((others,)),
             dma((others,)),
+            dma((mates,)),
+            dma((mates,)),
         ],
         compiler_params=pltpu.CompilerParams(
             collective_id=0, has_side_effects=True, vmem_limit_bytes=VMEM_BYTES
@@ -990,10 +1038,8 @@
 
 def on_device(features, ln_gain, w_qkv, qk_gain, w_up, w_out, w_down, cotangent):
     images, patches, width = features.shape
-    head_cols = w_qkv.shape[2]
-    qkv_flat = w_qkv.reshape(width, 3 * head_cols)
     output, input_grad, ln_grad, gains, qkv_units, up_grad, out_grad, down_grad = exchange(
-        qkv_flat, w_up, w_out, w_down, qk_gain, features, cotangent, ln_gain.reshape(1, width)
+        jnp.transpose(w_qkv, (1, 0, 2)), w_up, w_out, w_down, qk_gain, features, cotangent, ln_gain.reshape(1, width)
     )
     units = qkv_units.reshape(3, 2, width, HEAD)
     whole, split = units[:, 0], units[:, 1]
@@ -1005,7 +1051,7 @@
     )
     qkv_grad = jnp.transpose(qkv_grad, (1, 0, 2))
     return (
-        output, input_grad, ln_grad.reshape(width), gains[:2], qkv_grad, up_grad, out_grad, down_grad
+        output, input_grad, ln_grad, gains, qkv_grad, up_grad, out_grad, down_grad
     )
 
 

time: 259 us -> 247 us (0.954)
  Pallas kernels: 242 us -> 234 us
  local copies, waits for them, and re-layouts: 12.9 us -> 8.37 us
    pallas_call x1, Pallas kernels: 242 us -> 234 us  [exchange(): pl.pallas_call(functools.partial(core_kernel, dps, rows, cols), out_shape...]
    unnamed x20 -> x23, local copies, waits for them, and re-layouts: 7.37 us -> 5.76 us
where the time goes in v4:
time: 247 us; the launch traced here: 244 us
  Pallas kernels  234 us (95%)
  local copies, waits for them, and re-layouts  8.37 us (3%)
    pallas_call x1, Pallas kernels, exchange(): pl.pallas_call(functools.partial(core_kernel, dps, rows, cols), out_shape...  234 us
    unnamed x23, local copies, waits for them, and re-layouts  5.76 us

profile of v4, /device:TPU:1, one launch (start us, length us, event | category | flops | bytes accessed | tf_op | source)
XLA Modules:
  0.0 244.1 jit_solution(11443781323786442600)
XLA Ops:
  0.6 1.2 reshape.22.ln_ref
  1.9 234.0 %exchange.1 = (bf16[2,64,384]{2,1,0:T(8,128)(2,1)}, bf16[2,64,384]{2,1,0:T(8,128)(2,1)}, f32[384]{0:T(512)}, f32[2,128]{1,0:T(2,128)}, f32[6,384,128]{2,1,0:T(8,...) custom-call(bf16[3,384,768]{2,1,0:T(8,128)(2,1)} %bitcast.8, bf16[384,3072]{1,0:T(8,128)(2,1)} %wup_hbm.1, ...), custom_call_target="tpu_custom_call" | custom-call | tf_op jit(solution)/shard_map/exchange/pallas_call | solution.py:940
  235.9 1.3 fusion.1
  237.2 0.2 copy.19
  237.5 0.2 copy.18
  237.7 0.0 copy-start.4
  237.7 0.0 copy-start.3
  237.7 0.0 copy-start.5
  237.8 0.0 copy-start.6
  237.8 0.0 copy-start.1
  237.8 1.0 fusion
  238.8 0.0 copy-done.4
  238.8 0.6 copy.27
  239.4 0.0 copy-done.3
  239.4 0.6 copy.28
  240.0 0.0 copy-done.5
  240.0 0.6 copy.29
  240.6 0.0 copy-done.6
  240.6 0.6 copy.30
  241.2 0.0 copy-done.1
  241.2 1.0 copy.31
  242.2 0.1 copy-done.2
  242.3 0.7 copy.32
  243.0 1.0 copy.33
  (4 shorter events, 0.0 us)
Async XLA Ops:
  237.7 1.0 copy-start.4
  237.7 1.7 copy-start.3
  237.7 2.3 copy-start.5
  237.8 2.9 %copy-start.6 = (f32[2,128]{1,0:T(2,128)S(1)}, f32[2,128]{1,0:T(2,128)}, u32[]{:S(2)}) copy-start(f32[2,128]{1,0:T(2,128)} %get-tuple-element.39) | copy-start | bytes 3076
  237.8 3.4 %copy-start.1 = (f32[384,768]{1,0:T(8,128)S(1)}, f32[384,768]{1,0:T(8,128)}, u32[]{:S(2)}) copy-start(f32[384,768]{1,0:T(8,128)} %get-tuple-element.41) | copy-start | bytes 3538948
  241.2 1.1 copy-start.2
  241.2 1.8 copy-start

commit v5 on v4

--- a/solution.py
+++ b/solution.py
@@ -490,6 +490,12 @@
         return carry
 
     lax.fori_loop(0, PIECES, settle, 0)
+    for k in range(1, cols):
+        norm_copy(k).wait_send()
+    if rows > 1:
+        for w, ref in enumerate((c_ref, x_ref)):
+            for turn in range(3):
+                row_gather(w, ref, turn).wait_send()
     out_acc[...] = jnp.zeros_like(out_acc)
     norm_acc[...] = jnp.zeros_like(norm_acc)
 
@@ -533,28 +539,30 @@
     def small_span(u):
         return pl.ds(pl.multiple_of(u * half_width, half_width), half_width)
 
+    all_halves = pl.ds(0, UNITS * half_width)
+
     def dopp_right(u):
         return remote(
             opp.at[unit_span(u, 0)], dhalf_left.at[small_span(u)],
-            s_dopp.at[0, u], r_dhalf.at[0, u], dp_right,
+            s_dopp.at[0], r_dhalf.at[0, u], dp_right,
         )
 
     def dopp_left(u):
         return remote(
             opp.at[unit_span(u, 1)], dhalf_right.at[small_span(u)],
-            s_dopp.at[1, u], r_dhalf.at[1, u], dp_left,
+            s_dopp.at[1], r_dhalf.at[1, u], dp_left,
         )
 
     def dside_right(u, half):
         return remote(
             right_send.at[unit_span(u, half)], dfull_left.at[unit_span(u, half)],
-            s_dside.at[0, half, u], r_dfull.at[0, half, u], dp_right,
+            s_dside.at[0, half], r_dfull.at[0, half, u], dp_right,
         )
 
     def dside_left(u, half):
         return remote(
             left_send.at[unit_span(u, half)], dfull_right.at[unit_span(u, half)],
-            s_dside.at[1, half, u], r_dfull.at[1, half, u], dp_left,
+            s_dside.at[1, half], r_dfull.at[1, half, u], dp_left,
         )
 
     def emit_unit(dest, u, values):
@@ -670,7 +678,7 @@
     def passes(i):
         def each_pass(k, carry):
             block = lax.rem(xi + k, 4)
-            turn = i - 1 - jnp.where(k == 2, 2, 0)
+            turn = i - 2 - jnp.where(k == 2, 2, 0)
             p = piece_at(turn)
             live = (turn >= 0) & (turn < PIECES)
 
@@ -685,6 +693,11 @@
             return carry
 
         lax.fori_loop(0, SIDE, each_pass, 0)
+
+    def gathered(p):
+        for way in range(2):
+            own_ag(p, way).wait_send()
+            fwd_copy(p, way).wait_send()
 
     def step(i, carry):
         ahead = i + 2
@@ -733,8 +746,20 @@
             return carry
 
         lax.fori_loop(0, SIDE, each_block, 0)
-
         passes(i)
+
+        @pl.when((i >= 3) & (i < PIECES + 2))
+        def _():
+            gathered(piece_at(i - 3))
+
+        @pl.when(i == PIECES - 3)
+        def _():
+            gains = gain_mine[...]
+            for k in range(1, cols):
+                gain_copy(k).wait()
+                gains = gains + gain_in[k - 1]
+            last_mine[...] = gains
+
         return carry
 
     lax.fori_loop(0, STEPS, step, 0)
@@ -778,11 +803,6 @@
 
     for k in range(1, cols):
         stat_copy(k).start()
-    gains = gain_mine[...]
-    for k in range(1, cols):
-        gain_copy(k).wait_recv()
-        gains = gains + gain_in[k - 1]
-    last_mine[...] = gains
     runs = width // HEAD
     for j in range(runs):
         last_mine[2 + j : 3 + j, :] = ln_sum[:, j * HEAD : (j + 1) * HEAD]
@@ -792,8 +812,6 @@
             last_mine, last_in.at[k - 1], s_last.at[k - 1], r_last.at[k - 1], team_peer(k)
         )
 
-    for k in range(1, teams):
-        last_copy(k).start()
     if rows > 1:
         core_copy.wait_recv()
         for w in (1, 0):
@@ -802,7 +820,14 @@
                     row_part(accs[w], lax.rem(row + 2, rows), im) + core_in[0, w, im].astype(F32)
                 ).astype(BF16)
             row_copies[w].start()
-    passes(STEPS)
+    for k in range(1, teams):
+        last_copy(k).start()
+
+    def last_passes(i, carry):
+        passes(i)
+        return carry
+
+    lax.fori_loop(STEPS, STEPS + 2, last_passes, 0)
     for k in range(1, cols):
         stat_copy(k).wait_recv()
         stats = stats + stat_in[k - 1]
@@ -882,24 +907,16 @@
     for j in range(runs):
         ln_grad_ref[j * HEAD : (j + 1) * HEAD] = last[2 + j]
 
-    def finish(p, carry):
-        for way in range(2):
-            own_ag(p, way).wait_send()
-            fwd_copy(p, way).wait_send()
-        return carry
-
-    lax.fori_loop(0, PIECES, finish, 0)
-
-    def finish_unit(u, carry):
-        dopp_right(u).wait_send()
-        dopp_left(u).wait_send()
-        for half in range(2):
-            dside_right(u, half).wait_send()
-            dside_left(u, half).wait_send()
-        return carry
-
+    gathered(piece_at(PIECES - 1))
     if dps > 1:
-        lax.fori_loop(0, UNITS, finish_unit, 0)
+        for way, (send, there) in enumerate(((right_send, dp_right), (left_send, dp_left))):
+            remote(
+                opp.at[all_halves], dhalf_left, s_dopp.at[way], r_dhalf.at[way, 0], there
+            ).wait_send()
+            for half in range(2):
+                remote(
+                    send.at[all_halves], dhalf_left, s_dside.at[way, half], r_dhalf.at[way, 0], there
+                ).wait_send()
     for p in range(PIECES):
         pl.when(zi != owner_z(p))(lambda: chain_copy(p, True).wait_send())
         if owner_z(p) < 3:
@@ -908,19 +925,13 @@
             pl.when((zi <= owner_z(p)) & (zi > 0))(lambda: z_ag(p, False).wait_send())
 
     for k in range(1, cols):
-        gain_copy(k).wait_send()
         stat_copy(k).wait_send()
-    for k in range(1, cols):
-        norm_copy(k).wait_send()
     if rows > 1:
         core_copy.wait_send()
         for w in range(2):
             row_copies[w].wait_send()
         for k in range(1, rows):
             both_copy(k).wait_send()
-        for w, ref in enumerate((c_ref, x_ref)):
-            for turn in range(3):
-                row_gather(w, ref, turn).wait_send()
     for k in range(1, teams):
         last_copy(k).wait_send()
 
@@ -1014,9 +1025,9 @@
             dma((2, 3)),
             dma((1,)),
             dma((1,)),
+            dma((2,)),
             dma((2, UNITS)),
-            dma((2, UNITS)),
-            dma((2, 2, UNITS)),
+            dma((2, 2)),
             dma((2, 2, UNITS)),
             dma((2,)),
             dma((2,)),

time: 247 us -> 246 us (level)
  the two profiles are of different devices: /device:TPU:1 before, /device:TPU:25 now
where the time goes in v5:
time: 246 us; the launch traced here: 245 us
  Pallas kernels  235 us (96%)
  local copies, waits for them, and re-layouts  8.37 us (3%)
    pallas_call x1, Pallas kernels, exchange(): pl.pallas_call(functools.partial(core_kernel, dps, rows, cols), out_shape...  235 us
    unnamed x23, local copies, waits for them, and re-layouts  5.76 us

profile of v5, /device:TPU:25, one launch (start us, length us, event | category | flops | bytes accessed | tf_op | source)
XLA Modules:
  0.0 245.4 jit_solution(8706788804953841821)
XLA Ops:
  0.6 1.2 reshape.22.ln_ref
  1.9 235.4 %exchange.1 = (bf16[2,64,384]{2,1,0:T(8,128)(2,1)}, bf16[2,64,384]{2,1,0:T(8,128)(2,1)}, f32[384]{0:T(512)}, f32[2,128]{1,0:T(2,128)}, f32[6,384,128]{2,1,0:T(8,...) custom-call(bf16[3,384,768]{2,1,0:T(8,128)(2,1)} %bitcast.8, bf16[384,3072]{1,0:T(8,128)(2,1)} %wup_hbm.1, ...), custom_call_target="tpu_custom_call" | custom-call | tf_op jit(solution)/shard_map/exchange/pallas_call | solution.py:951
  237.3 1.3 fusion.1
  238.6 0.2 copy.19
  238.9 0.2 copy.18
  239.1 0.0 copy-start.4
  239.1 0.0 copy-start.3
  239.1 0.0 copy-start.5
  239.1 0.0 copy-start.6
  239.1 0.0 copy-start.1
  239.2 1.0 fusion
  240.1 0.0 copy-done.4
  240.1 0.6 copy.27
  240.8 0.0 copy-done.3
  240.8 0.6 copy.28
  241.4 0.0 copy-done.5
  241.4 0.6 copy.29
  242.0 0.0 copy-done.6
  242.0 0.6 copy.30
  242.6 0.0 copy-done.1
  242.6 1.0 copy.31
  243.6 0.1 copy-done.2
  243.7 0.7 copy.32
  244.4 1.0 copy.33
  (4 shorter events, 0.0 us)
Async XLA Ops:
  239.1 1.0 copy-start.4
  239.1 1.7 copy-start.3
  239.1 2.3 copy-start.5
  239.1 2.9 %copy-start.6 = (f32[2,128]{1,0:T(2,128)S(1)}, f32[2,128]{1,0:T(2,128)}, u32[]{:S(2)}) copy-start(f32[2,128]{1,0:T(2,128)} %get-tuple-element.39) | copy-start | bytes 3076
  239.1 3.4 %copy-start.1 = (f32[384,768]{1,0:T(8,128)S(1)}, f32[384,768]{1,0:T(8,128)}, u32[]{:S(2)}) copy-start(f32[384,768]{1,0:T(8,128)} %get-tuple-element.41) | copy-start | bytes 3538948
  242.6 1.1 copy-start.2
  242.6 1.8 copy-start

commit v6 on v5

--- a/solution.py
+++ b/solution.py
@@ -827,7 +827,6 @@
         passes(i)
         return carry
 
-    lax.fori_loop(STEPS, STEPS + 2, last_passes, 0)
     for k in range(1, cols):
         stat_copy(k).wait_recv()
         stats = stats + stat_in[k - 1]
@@ -839,6 +838,8 @@
 
     for k in range(1, rows):
         both_copy(k).start()
+
+    lax.fori_loop(STEPS, STEPS + 2, last_passes, 0)
 
     def row_total(w, acc):
         parts = []

time: 246 us -> 246 us (level)
  the two profiles are of different devices: /device:TPU:25 before, /device:TPU:1 now
where the time goes in v6:
time: 246 us; the launch traced here: 241 us
  Pallas kernels  231 us (94%)
  local copies, waits for them, and re-layouts  8.37 us (3%)
    pallas_call x1, Pallas kernels, exchange(): pl.pallas_call(functools.partial(core_kernel, dps, rows, cols), out_shape...  231 us
    unnamed x23, local copies, waits for them, and re-layouts  5.76 us

profile of v6, /device:TPU:1, one launch (start us, length us, event | category | flops | bytes accessed | tf_op | source)
XLA Modules:
  0.0 241.4 jit_solution(9888385635959463695)
XLA Ops:
  0.6 1.2 reshape.22.ln_ref
  1.9 231.3 %exchange.1 = (bf16[2,64,384]{2,1,0:T(8,128)(2,1)}, bf16[2,64,384]{2,1,0:T(8,128)(2,1)}, f32[384]{0:T(512)}, f32[2,128]{1,0:T(2,128)}, f32[6,384,128]{2,1,0:T(8,...) custom-call(bf16[3,384,768]{2,1,0:T(8,128)(2,1)} %bitcast.8, bf16[384,3072]{1,0:T(8,128)(2,1)} %wup_hbm.1, ...), custom_call_target="tpu_custom_call" | custom-call | tf_op jit(solution)/shard_map/exchange/pallas_call | solution.py:952
  233.2 1.3 fusion.1
  234.6 0.2 copy.19
  234.8 0.2 copy.18
  235.1 0.0 copy-start.4
  235.1 0.0 copy-start.3
  235.1 0.0 copy-start.5
  235.1 0.0 copy-start.6
  235.1 0.0 copy-start.1
  235.1 1.0 fusion
  236.1 0.0 copy-done.4
  236.1 0.6 copy.27
  236.7 0.0 copy-done.3
  236.7 0.6 copy.28
  237.4 0.0 copy-done.5
  237.4 0.6 copy.29
  238.0 0.0 copy-done.6
  238.0 0.6 copy.30
  238.5 0.0 copy-done.1
  238.5 1.0 copy.31
  239.6 0.1 copy-done.2
  239.7 0.7 copy.32
  240.4 1.0 copy.33
  (4 shorter events, 0.0 us)
Async XLA Ops:
  235.1 1.0 copy-start.4
  235.1 1.7 copy-start.3
  235.1 2.3 copy-start.5
  235.1 2.9 %copy-start.6 = (f32[2,128]{1,0:T(2,128)S(1)}, f32[2,128]{1,0:T(2,128)}, u32[]{:S(2)}) copy-start(f32[2,128]{1,0:T(2,128)} %get-tuple-element.39) | copy-start | bytes 3076
  235.1 3.4 %copy-start.1 = (f32[384,768]{1,0:T(8,128)S(1)}, f32[384,768]{1,0:T(8,128)}, u32[]{:S(2)}) copy-start(f32[384,768]{1,0:T(8,128)} %get-tuple-element.41) | copy-start | bytes 3538948
  238.5 1.1 copy-start.2
  238.5 1.8 copy-start
